TPU v7x, 128 devices: a whole 4x4x4 slice. The times are simulated.
128 devices in a mesh: dp: 4 (over y), expert: 8 (over z, core), tensor: 4 (over x).
Axes of the slice: x: 4, y: 4, z: 4, core: 2. Of those that a mesh axis runs over, the one named last changes fastest.
Arguments:
- tokens: bfloat16 [16384, 1536], P(('dp', 'expert', 'tensor')), may hold values from -6 to 6
- documents: int32 [16384], P(('dp', 'expert')), may hold values from 0 to 2, as said below
- expert_routes: int32 [16384, 8], P(('dp', 'expert', 'tensor')), may hold values from 0 to 39, all different within a row; in each aligned block of 128 rows (0 to 127, 128 to 255, ...) at most 36 rows name the same one
- attention_gain: bfloat16 [1536], replicated, may hold values from 0.5 to 1.5
- query_weight: bfloat16 [1536, 1536], P(None, 'tensor'), may hold values from -0.15625 to 0.15625
- key_matrix: bfloat16 [1536, 512], P(None, 'tensor'), may hold values from -0.15625 to 0.15625
- value_matrix: bfloat16 [1536, 512], P(None, 'tensor'), may hold values from -0.15625 to 0.15625
- output_weight: bfloat16 [1536, 1536], P('tensor'), may hold values from -1.25 to 1.25
- expert_gain: bfloat16 [1536], replicated, may hold values from 0.5 to 1.5
- router_weight: bfloat16 [1536, 40], replicated, may hold values from -0.078125 to 0.078125
- gate_weight: bfloat16 [40, 1536, 512], P('expert', None, 'tensor'), may hold values from -0.15625 to 0.15625
- up_weight: bfloat16 [40, 1536, 512], P('expert', None, 'tensor'), may hold values from -0.15625 to 0.15625
- down_weight: bfloat16 [40, 512, 1536], P('expert', 'tensor'), may hold values from -1 to 1
- out_cotangent: bfloat16 [16384, 1536], P(('dp', 'expert', 'tensor')), may hold values from -6 to 6
Outputs:
- layer_output: bfloat16 [16384, 1536], P(('dp', 'expert', 'tensor'))
- input_gradient: float32 [16384, 1536], P(('dp', 'expert', 'tensor'))
- attention_gain_gradient: float32 [1536], replicated
- query_gradient: float32 [1536, 1536], P(None, 'tensor')
- key_gradient: float32 [1536, 512], P(None, 'tensor')
- value_gradient: float32 [1536, 512], P(None, 'tensor')
- output_gradient: float32 [1536, 1536], P('tensor')
- expert_gain_gradient: float32 [1536], replicated
- router_gradient: float32 [1536, 40], replicated
- gate_gradient: float32 [40, 1536, 512], P('expert', None, 'tensor')
- up_gradient: float32 [40, 1536, 512], P('expert', None, 'tensor')
- down_gradient: float32 [40, 512, 1536], P('expert', 'tensor')
Inputs may be any that keep to these rules, and one draw needn't show every extreme that they name: `documents`: in each group of 512 consecutive tokens the ids never fall and begin at 0. `expert_routes`: each token names 8 different experts; among the pairs of the 128 tokens of one device no expert is named more than 36 times.
All inputs are finite; a program needn't handle non-finite values.
Results may differ from a plain program's by a relative error of at most 0.025.
Values may be sent and summed in bfloat16 or wider, within the bound.
A program may use at most 384 MiB of HBM per device.

v0:
```python
import functools

import jax
import jax.numpy as jnp
from jax import lax
from jax.experimental import pallas as pl
from jax.experimental.pallas import tpu as pltpu
from jax.sharding import PartitionSpec as P


epsilon = 1e-06
highest = lax.Precision.HIGHEST


def normalize(value_rows, gain):
    scale = lax.rsqrt(jnp.mean(value_rows * value_rows, -1, keepdims=True) + epsilon)
    return (value_rows * scale * gain, scale)


def norm_back(value_rows, scale, gain, upstream):
    weighted = upstream * gain
    inner = jnp.mean(weighted * value_rows, -1, keepdims=True)
    result = scale * weighted - value_rows * scale**3 * inner
    gain_part = jnp.sum(upstream * value_rows * scale, 0)
    return (result, gain_part)


MESH = pl.DeviceIdType.MESH

NT = (((1,), (1,)), ((), ()))
TN = (((0,), (0,)), ((), ()))


def turn(v, cosine, sine):
    lane = lax.broadcasted_iota(jnp.int32, v.shape, 1)
    count = v.shape[1]
    partner = jnp.where(lane % 64 < 32, pltpu.roll(v, count - 32, 1), pltpu.roll(v, 32, 1))
    times = count // 128
    return v * jnp.concatenate([cosine] * times, 1) + partner * jnp.concatenate([sine] * times, 1)


def attend(group, gain, cosine, sine, bias, wq, wk, wv, wo, rows_ref, q_ref, k_ref, v_ref, mixed_ref, logsum_ref, part_ref):
    f32, low = jnp.float32, jnp.bfloat16
    t = group[...].reshape(512, 1536).astype(f32)
    scale = lax.rsqrt(jnp.mean(t * t, -1, keepdims=True) + epsilon)
    rows_ref[...] = (t * scale * gain[...]).astype(low)
    rows = rows_ref[...]
    cos, sin = cosine[...], sine[...]
    q_ref[...] = (turn(jnp.dot(rows, wq[...], preferred_element_type=f32), cos, sin) * 0.125).astype(low)
    k_ref[...] = turn(jnp.dot(rows, wk[...], preferred_element_type=f32), cos, sin).astype(low)
    v_ref[...] = jnp.dot(rows, wv[...], preferred_element_type=f32).astype(low)
    lane = lax.broadcasted_iota(jnp.int32, (512, 128), 1)
    logsum = jnp.zeros((512, 128), f32)
    for h in range(6):
        kv = slice(64 * (h // 3), 64 * (h // 3) + 64)
        s = lax.dot_general(q_ref[:, 64 * h : 64 * h + 64], k_ref[:, kv], NT, preferred_element_type=f32) + bias[...]
        top = jnp.max(s, -1, keepdims=True)
        p = jnp.exp(s - top)
        total = jnp.sum(p, -1, keepdims=True)
        mixed = jnp.dot(p.astype(low), v_ref[:, kv], preferred_element_type=f32) / total
        mixed_ref[:, 64 * h : 64 * h + 64] = mixed.astype(low)
        logsum = jnp.where(lane == h, top + jnp.log(total), logsum)
    logsum_ref[...] = logsum
    part_ref[...] = jnp.dot(mixed_ref[...], wo[...], preferred_element_type=f32).astype(low).reshape(4, 128, 1536)


def weight_loads(gate, up, router, w, sem):
    return (
        [pltpu.make_async_copy(gate.at[n], w.at[:, pl.ds(128 * n, 128)], sem.at[n]) for n in range(5)]
        + [pltpu.make_async_copy(up.at[n], w.at[:, pl.ds(640 + 128 * n, 128)], sem.at[5 + n]) for n in range(5)]
        + [pltpu.make_async_copy(router, w.at[:, pl.ds(1280, 128)], sem.at[10])]
    )


PAIRS = ((0, 0), (1, 0), (3, 0), (0, 1), (0, 3), (2, 0), (0, 2), (1, 1), (1, 3), (3, 1), (3, 3), (2, 1), (2, 3), (1, 2), (3, 2), (2, 2))


class PlaneGather:
    def __init__(self, place, own, peer, sibling, core, send_sem, recv_sem, sib_send, sib_recv, starts, by_columns=False):
        self.starts, self.by_columns = starts, by_columns
        self.place, self.own, self.peer, self.sibling, self.core = place, own, peer, sibling, core
        self.send_sem, self.recv_sem, self.sib_send, self.sib_recv = send_sem, recv_sem, sib_send, sib_recv
        self.later = []

    def copy(self, dx, dz, ox, oz, q, nq, n, own):
        quarter = pl.ds(self.starts[q], self.starts[q + nq] - self.starts[q])
        quarter = (slice(None), quarter) if self.by_columns else quarter
        there = self.place(dx, dz, self.core).at[quarter]
        return pltpu.make_async_remote_copy(
            src_ref=self.own.at[quarter] if own and self.own is not None else there, dst_ref=there,
            send_sem=self.send_sem.at[n], recv_sem=self.recv_sem.at[(dx - ox) % 4, (dz - oz) % 4, q],
            device_id=self.peer(ox, oz), device_id_type=MESH)

    def send(self, dx, dz, ox, oz, q, nq, own=False):
        if self.starts[q] == self.starts[q + nq]:
            return
        make = functools.partial(self.copy, dx, dz, ox, oz, q, nq, len(self.later), own)
        make().start()
        self.later.append(make)

    def recv(self, dx, dz, q, nq):
        if self.starts[q] == self.starts[q + nq]:
            return
        self.copy(dx, dz, 0, 0, q, nq, 0, False).wait_recv()

    def sib_copy(self, core, dx, dz, own=False):
        there = self.place(dx, dz, core)
        return pltpu.make_async_remote_copy(
            src_ref=self.own if own else there, dst_ref=there,
            send_sem=self.sib_send.at[dx % 4, dz % 4], recv_sem=self.sib_recv.at[dx % 4, dz % 4],
            device_id=self.sibling, device_id_type=MESH)

    def sib_pass(self, dx, dz, own=False):
        make = functools.partial(self.sib_copy, self.core, dx, dz, own)
        make().start()
        self.later.append(make)

    def start(self, directions):
        for ox, oz in directions:
            self.send(0, 0, ox, oz, 0, 4, own=True)

    def wave1x(self):
        for s in (1, -1):
            self.recv(s, 0, 0, 4)
            if s == -1:
                self.send(s, 0, 1, 0, 1, 2)
            else:
                self.send(s, 0, -1, 0, 0, 1)
                self.send(s, 0, -1, 0, 3, 1)
            for oz in (1, -1):
                self.send(s, 0, 0, oz, 0, 2)
            self.sib_pass(s, 0)

    def wave1z(self):
        for s in (1, -1):
            self.recv(0, s, 0, 4)
            if s == -1:
                self.send(0, s, 0, 1, 1, 2)
            else:
                self.send(0, s, 0, -1, 0, 1)
                self.send(0, s, 0, -1, 3, 1)
            for ox in (1, -1):
                self.send(0, s, ox, 0, 2, 2)
            self.sib_pass(0, s)

    def wave1(self):
        self.wave1x()
        self.wave1z()

    def wave2(self):
        for q, nq in ((1, 2), (0, 1), (3, 1)):
            self.recv(2, 0, q, nq)
        for oz in (1, -1):
            self.send(2, 0, 0, oz, 0, 2)
        for q, nq in ((1, 2), (0, 1), (3, 1)):
            self.recv(0, 2, q, nq)
        for ox in (1, -1):
            self.send(0, 2, ox, 0, 2, 2)
        self.sib_pass(2, 0)
        self.sib_pass(0, 2)
        for dx in (1, -1):
            for s in (1, -1):
                self.recv(dx, s, 0, 2)
                self.send(dx, s, 0, -s, 0 if s == 1 else 1, 1)
                self.recv(s, dx, 2, 2)
                self.send(s, dx, -s, 0, 2 if s == 1 else 3, 1)
        for dx in (1, -1):
            for dz in (1, -1):
                self.sib_pass(dx, dz)

    def wave3(self):
        for s in (1, -1):
            self.recv(2, s, 0, 2)
            self.send(2, s, 0, -s, 0 if s == 1 else 1, 1)
            self.recv(s, 2, 2, 2)
            self.send(s, 2, -s, 0, 2 if s == 1 else 3, 1)
        for d in (1, -1):
            for q in (0, 1):
                self.recv(d, 2, q, 1)
                self.recv(2, d, q + 2, 1)
        for d in (1, -1):
            self.sib_pass(d, 2)
            self.sib_pass(2, d)

    def wave4(self):
        for q in range(4):
            self.recv(2, 2, q, 1)
        self.sib_pass(2, 2)

    def finish(self):
        for make in self.later:
            make().wait_send()


def front_kernel(tokens, u_own, first_gain, second_gain, cosine, sine, bias, wq, wk, wv, wo, gate_hbm, up_hbm, router_hbm, down_hbm,
                 residual, rows_out, acts_out, u_hbm, group, normed, queries, keys, values, mixed, logsum,
                 part, nr1, nb, nr2, rows, w, down, u_buf, act_buf,
                 gsend, grecv, own_sem, nsend, nrecv, send_sem, recv_sem, sib_send, sib_recv,
                 u_send, u_recv, u_sib_send, u_sib_recv, w_sem, down_sem, u_sem, act_sem, out_sem):
    f32, low = jnp.float32, jnp.bfloat16
    wide = 640
    width = 1536
    x = lax.axis_index("tensor"); e = lax.axis_index("expert")
    z = e // 2; c = e % 2
    first = e * 5
    def xi(d): return (x + d) % 4
    def zi(d): return (z + d) % 4
    def peer(ox, oz):
        return {"expert": zi(oz) * 2 + c, "tensor": xi(ox)}
    sib = {"expert": z * 2 + 1 - c}
    def pair(step):
        if isinstance(step, int):
            return PAIRS[step]
        dx = dz = 0
        for n in range(4):
            here = lax.convert_element_type(step // 4 == n, jnp.int32)
            dx = dx + here * sum(PAIRS[4 * n + m][0] * 4**m for m in range(4))
            dz = dz + here * sum(PAIRS[4 * n + m][1] * 4**m for m in range(4))
        for n in range(3):
            more = lax.convert_element_type(step % 4 > n, jnp.int32)
            dx = dx // (1 + 3 * more)
            dz = dz // (1 + 3 * more)
        dx, dz = dx % 4, dz % 4
        return dx, dz
    def u_loads(step):
        dx, dz = pair(step)
        return pltpu.make_async_copy(u_hbm.at[zi(dz), xi(dx)], u_buf.at[step % 2], u_sem.at[step % 2])
    loads = weight_loads(gate_hbm, up_hbm, router_hbm, w, w_sem) + [pltpu.make_async_copy(down_hbm, down, down_sem)]
    for cp in loads: cp.start()
    barrier = pltpu.get_barrier_semaphore()
    near = [peer(1, 0), peer(-1, 0), peer(0, 1), peer(0, -1), sib]
    for p in near:
        pl.semaphore_signal(barrier, inc=1, device_id=p, device_id_type=MESH)
    pl.semaphore_wait(barrier, len(near))
    pend = []
    def go(cps):
        for cp in cps: cp.start()
        pend.extend(cps)
        return cps
    def block_of(ref):
        return lambda dx, dz, core: ref.at[zi(dz), xi(dx), core]
    cots = PlaneGather(block_of(u_hbm), u_own, peer, sib, c, u_send, u_recv, u_sib_send, u_sib_recv, (0, 48, 96, 112, 128))
    norms = PlaneGather(block_of(rows), rows.at[z, x, c], peer, sib, c, send_sem, recv_sem, sib_send, sib_recv, (0, 16, 32, 80, 128))
    def tok(n, block, half, to, own):
        there = group.at[block, pl.ds(64 * half, 64)]
        return pltpu.make_async_remote_copy(
            src_ref=tokens.at[pl.ds(64 * half, 64)] if own else there, dst_ref=there,
            send_sem=gsend.at[n], recv_sem=grecv.at[n], device_id=peer(to, 0), device_id_type=MESH)
    go([tok(0, x, 0, 1, True), tok(2, x, 1, -1, True)])
    go([tok(1, x, 1, 1, True), tok(3, x, 0, -1, True)])
    mine = pltpu.make_async_copy(u_own, u_hbm.at[z, x, c], own_sem)
    mine.start()
    cots.start(((0, 1), (0, -1)))
    group[x] = tokens[...]
    tok(0, xi(-1), 0, 1, False).wait_recv()
    go([tok(4, xi(-1), 0, 1, False)])
    tok(2, xi(1), 1, -1, False).wait_recv()
    go([tok(5, xi(1), 1, -1, False)])
    cots.start(((1, 0), (-1, 0)))
    cots.sib_pass(0, 0, own=True)
    tok(1, xi(-1), 1, 1, False).wait_recv()
    tok(3, xi(1), 0, -1, False).wait_recv()
    tok(4, xi(2), 0, 1, False).wait_recv()
    tok(5, xi(2), 1, -1, False).wait_recv()
    attend(group, first_gain, cosine, sine, bias, wq, wk, wv, wo, normed, queries, keys, values, mixed, logsum, part)
    def nrc(n, src, dst, to):
        return pltpu.make_async_remote_copy(src_ref=src, dst_ref=dst, send_sem=nsend.at[n], recv_sem=nrecv.at[n],
                                            device_id=peer(to, 0), device_id_type=MESH)
    n1 = go([nrc(0, part.at[xi(2), pl.ds(0, 64)], nr1.at[0], 1), nrc(1, part.at[xi(2), pl.ds(64, 64)], nr1.at[1], -1)])
    n2 = go([nrc(2, part.at[xi(1), pl.ds(64, 64)], nr2.at[0, pl.ds(64, 64)], 1),
             nrc(3, part.at[xi(-1), pl.ds(0, 64)], nr2.at[1, pl.ds(0, 64)], -1)])
    cots.wave1()
    mine.wait()
    cots.sib_copy(1 - c, 0, 0).wait_recv()
    u_loads(0).start()
    n1[0].wait_recv()
    nb[0] = (part[xi(1), 0:64].astype(f32) + nr1[0].astype(f32)).astype(low)
    n3 = go([nrc(4, nb.at[0], nr2.at[0, pl.ds(0, 64)], 1)])
    n1[1].wait_recv()
    nb[1] = (part[xi(-1), 64:128].astype(f32) + nr1[1].astype(f32)).astype(low)
    n3 += go([nrc(5, nb.at[1], nr2.at[1, pl.ds(64, 64)], -1)])
    for cp in n2 + n3: cp.wait_recv()
    total = tokens[...].astype(f32) + part[x].astype(f32) + nr2[0].astype(f32) + nr2[1].astype(f32)
    residual[...] = total
    scale = lax.rsqrt(jnp.mean(total * total, -1, keepdims=True) + epsilon)
    rows[z, x, c] = (total * scale * second_gain[...]).astype(low)
    norms.start(((1, 0), (-1, 0), (0, 1), (0, -1)))
    norms.sib_pass(0, 0, own=True)
    for cp in loads: cp.wait()

    def act_store(step):
        dx, dz = pair(step)
        return pltpu.make_async_copy(act_buf.at[step % 2], acts_out.at[zi(dz), xi(dx)].reshape(256, 2048), act_sem.at[step % 2])
    def row_store(step):
        dx, dz = pair(step)
        there = (zi(dz), xi(dx))
        return pltpu.make_async_copy(rows.at[there], rows_out.at[there], out_sem.at[step])
    def compute(step):
        dx, dz = pair(step)
        norms.sib_copy(1 - c, dx, dz).wait_recv()
        u_loads(step).wait()
        @pl.when(step < 15)
        def _():
            nx, nz = pair(step + 1)
            cots.sib_copy(1 - c, nx, nz).wait_recv()
            u_loads(step + 1).start()
        row_store(step).start()
        @pl.when(step >= 2)
        def _(): act_store(step - 2).wait()
        slot = step % 2
        here = act_buf.at[slot]
        pre = jnp.dot(rows[zi(dz), xi(dx)].reshape(256, width), w[...], preferred_element_type=f32)
        raw = lax.dot_general(u_buf[slot, :, :, 0:width].reshape(256, width), down[...], (((1,), (1,)), ((), ())), preferred_element_type=f32)
        lane = lax.broadcasted_iota(jnp.int32, (256, 128), 1)
        routes = u_buf[slot, :, :, width:].reshape(256, 128).astype(f32).astype(jnp.int32)
        named = lane == routes[:, 0:1]
        for n in range(1, 8):
            named = named | (lane == routes[:, n : n + 1])
        logits = jnp.where(named, pre[:, 2 * wide :], -1e30)
        raised = jnp.exp(logits - jnp.max(logits, -1, keepdims=True))
        gates = raised / jnp.sum(raised, -1, keepdims=True)
        weighted = jnp.zeros((256, 128), f32)
        for n in range(5):
            cols = slice(128 * n, 128 * (n + 1))
            gate = jnp.sum(jnp.where(lane == first + n, gates, 0.0), -1, keepdims=True)
            gate_pre = pre[:, cols]
            up_pre = pre[:, wide + 128 * n : wide + 128 * (n + 1)]
            sig = jax.nn.sigmoid(gate_pre)
            silu = gate_pre * sig
            active = silu * up_pre
            back = raw[:, cols]
            share = gate * jnp.sum(active * back, -1, keepdims=True)
            high = share.astype(low).astype(f32)
            weighted = weighted + jnp.where(lane == first + n, high, 0.0)
            weighted = weighted + jnp.where(lane == first + n + 64, share - high, 0.0)
            back = gate * back
            here[:, cols] = (gate * active).astype(low)
            here[:, wide + 128 * n : wide + 128 * (n + 1)] = (
                back * up_pre * (sig * (1.0 + gate_pre * (1.0 - sig)))
            ).astype(low)
            here[:, 2 * wide + 128 * n : 2 * wide + 128 * (n + 1)] = (back * silu).astype(low)
        here[:, 3 * wide :] = weighted.astype(low)
        act_store(step).start()

    events = ((0, cots.wave2), (1, norms.wave1), (3, cots.wave3), (5, norms.wave2), (7, cots.wave4), (9, norms.wave3), (13, norms.wave4))
    def body(step, _):
        for at, wave in events:
            @pl.when(step == at)
            def _():
                wave()
        compute(step)
        return 0
    lax.fori_loop(0, 16, body, 0)
    act_store(14).wait()
    act_store(15).wait()
    for n in range(16): row_store(n).wait()
    for cp in pend: cp.wait_send()
    cots.finish()
    norms.finish()


def front(tokens, u, first_gain, second_gain, cosine, sine, bias, wq, wk, wv, wo, gate, up, router, down, cid):
    bf, f32 = jnp.bfloat16, jnp.float32
    V = pltpu.VMEM
    D = pltpu.SemaphoreType.DMA
    S = jax.ShapeDtypeStruct
    vm = pl.BlockSpec(memory_space=pltpu.VMEM)
    anym = pl.BlockSpec(memory_space=pl.ANY)
    n, width = tokens.shape
    return pl.pallas_call(
        front_kernel,
        out_shape=(S((n, width), f32), S((4, 4, 2, n, width), bf), S((4, 4, 2, n, 2048), bf), S((4, 4, 2, n, 1664), bf),
                   S((4, n, width), bf), S((512, width), bf), S((512, 384), bf), S((512, 128), bf), S((512, 128), bf),
                   S((512, 384), bf), S((512, 128), f32)),
        in_specs=[vm, anym] + [vm] * 9 + [anym] * 4,
        out_specs=(vm, anym, anym, anym) + (vm,) * 7,
        scratch_shapes=[V((4, n, width), bf), V((2, 64, width), bf), V((2, 64, width), bf), V((2, 128, width), bf),
                        V((4, 4, 2, n, width), bf), V((width, 1408), bf), V((640, width), bf),
                        V((2, 2, n, 1664), bf), V((2, 256, 2048), bf),
                        D((6,)), D((6,)), D(()), D((6,)), D((6,)), D((64,)), D((4, 4, 4)), D((4, 4)), D((4, 4)),
                        D((64,)), D((4, 4, 4)), D((4, 4)), D((4, 4)),
                        D((11,)), D(()), D((2,)), D((2,)), D((16,))],
        compiler_params=pltpu.CompilerParams(collective_id=cid, has_side_effects=True, vmem_limit_bytes=60 << 20),
        name="front",
    )(tokens, u, first_gain, second_gain, cosine, sine, bias, wq, wk, wv, wo, gate, up, router, down)


class TorusSum:
    def __init__(self, g, out, scratch, sems, starts, place, with_extra):
        self.with_extra = with_extra
        (self.q, self.sib, self.a3, self.a3b, self.b3, self.b3b, self.a4, self.b4,
         self.a5, self.a5b, self.b5, self.b5b, self.a6, self.b6, self.extra) = scratch
        self.ssem, self.rsem, gsend, grecv, gsib_send, gsib_recv = sems
        self.g, self.out = g, out
        self.z, self.y, self.c, self.zi, self.yi, self.peer, self.xpeer, self.partner = place
        self.parts = [pl.ds(starts[n], starts[n + 1] - starts[n]) for n in range(4)]
        self.A = pl.ds(0, starts[2])
        self.B = pl.ds(starts[2], starts[4] - starts[2])
        self.sent = []
        self.back = PlaneGather(
            lambda dy, dz, core: out.at[core, self.zi(dz), self.yi(dy)], None, lambda oy, oz: self.peer(oz, oy), self.partner, self.c,
            gsend, grecv, gsib_send, gsib_recv, starts, True)

    def rc(self, n, src, dst, to):
        return pltpu.make_async_remote_copy(src_ref=src, dst_ref=dst, send_sem=self.ssem.at[n], recv_sem=self.rsem.at[n],
                                            device_id=to, device_id_type=MESH)

    def go(self, cps):
        for cp in cps:
            cp.start()
        self.sent.extend(cps)
        return cps

    def add(self, i, j, cols, *terms):
        t = self.q[i, j, :, cols].astype(jnp.float32)
        for s in terms:
            t = t + s.astype(jnp.float32)
        self.q[i, j, :, cols] = t.astype(jnp.bfloat16)

    def stage1(self):
        self.c1 = self.go([self.rc(16, self.g.at[1 - self.c], self.sib, self.partner)])

    def stage2(self):
        q, zi, yi, peer = self.q, self.zi, self.yi, self.peer
        A0, A1, B0, B1 = self.parts
        self.c1[0].wait_recv()
        def body(n, _):
            i, j = n // 4, n % 4
            q[i, j] = (self.g[self.c, i, j].astype(jnp.float32) + self.sib[i, j].astype(jnp.float32)).astype(jnp.bfloat16)
            return 0
        lax.fori_loop(0, 16, body, 0)
        self.c3 = self.go([self.rc(0, q.at[zi(2), :, :, A0], self.a3, peer(1, 0)),
                           self.rc(1, q.at[zi(2), :, :, A1], self.a3b, peer(-1, 0)),
                           self.rc(2, q.at[:, yi(2), :, B0], self.b3, peer(0, 1)),
                           self.rc(3, q.at[:, yi(2), :, B1], self.b3b, peer(0, -1))])

    def stage4(self):
        q, zi, yi, peer, A, B = self.q, self.zi, self.yi, self.peer, self.A, self.B
        A0, A1, B0, B1 = self.parts
        for cp in self.c3: cp.wait_recv()
        def body(n, _):
            self.add(zi(1), n, A0, self.a3[n])
            self.add(zi(-1), n, A1, self.a3b[n])
            self.add(n, yi(1), B0, self.b3[n])
            self.add(n, yi(-1), B1, self.b3b[n])
            return 0
        lax.fori_loop(0, 4, body, 0)
        self.c4 = self.go([self.rc(4, q.at[zi(1), :, :, A], self.a4.at[0], peer(1, 0)),
                           self.rc(5, q.at[zi(-1), :, :, A], self.a4.at[1], peer(-1, 0)),
                           self.rc(6, q.at[:, yi(1), :, B], self.b4.at[0], peer(0, 1)),
                           self.rc(7, q.at[:, yi(-1), :, B], self.b4.at[1], peer(0, -1))])

    def stage5(self):
        q, z, y, zi, yi, peer = self.q, self.z, self.y, self.zi, self.yi, self.peer
        A0, A1, B0, B1 = self.parts
        for cp in self.c4: cp.wait_recv()
        def body(n, _):
            self.add(z, n, self.A, self.a4[0, n], self.a4[1, n])
            self.add(n, y, self.B, self.b4[0, n], self.b4[1, n])
            return 0
        lax.fori_loop(0, 4, body, 0)
        self.c5 = self.go([self.rc(8, q.at[z, yi(2), :, A0], self.a5, peer(0, 1)),
                           self.rc(9, q.at[z, yi(2), :, A1], self.a5b, peer(0, -1)),
                           self.rc(10, q.at[zi(2), y, :, B0], self.b5, peer(1, 0)),
                           self.rc(11, q.at[zi(2), y, :, B1], self.b5b, peer(-1, 0))])

    def stage6(self):
        q, z, y, zi, yi, peer, A, B = self.q, self.z, self.y, self.zi, self.yi, self.peer, self.A, self.B
        A0, A1, B0, B1 = self.parts
        for cp in self.c5: cp.wait_recv()
        self.add(z, yi(1), A0, self.a5[...])
        self.add(z, yi(-1), A1, self.a5b[...])
        self.add(zi(1), y, B0, self.b5[...])
        self.add(zi(-1), y, B1, self.b5b[...])
        self.c6 = self.go([self.rc(12, q.at[z, yi(1), :, A], self.a6.at[0], peer(0, 1)),
                           self.rc(13, q.at[z, yi(-1), :, A], self.a6.at[1], peer(0, -1)),
                           self.rc(14, q.at[zi(1), y, :, B], self.b6.at[0], peer(1, 0)),
                           self.rc(15, q.at[zi(-1), y, :, B], self.b6.at[1], peer(-1, 0))])

    def stage7(self):
        f32, low = jnp.float32, jnp.bfloat16
        q, z, y = self.q, self.z, self.y
        for cp in self.c6: cp.wait_recv()
        own = self.out.at[self.c, z, y]
        own[:, self.A] = (q[z, y, :, self.A].astype(f32) + self.a6[0].astype(f32) + self.a6[1].astype(f32)).astype(low)
        last = (q[z, y, :, self.B].astype(f32) + self.b6[0].astype(f32) + self.b6[1].astype(f32)).astype(low)
        wide = last.shape[1] - (128 if self.with_extra else 0)
        own[:, pl.ds(self.B.start, wide)] = last[:, 0:wide]
        if not self.with_extra:
            return
        self.extra[0] = last[:, wide:]
        self.cx = self.go([self.rc(16 + o, self.extra.at[0], self.extra.at[o], self.xpeer(o)) for o in (1, 2, 3)])

    def start_back(self):
        f32 = jnp.float32
        if self.with_extra:
            for cp in self.cx: cp.wait_recv()
            extra = self.extra
            total = extra[0].astype(f32) + extra[1].astype(f32) + extra[2].astype(f32) + extra[3].astype(f32)
            self.out[self.c, self.z, self.y, :, pl.ds(self.B.start + self.B.size - 128, 128)] = total.astype(jnp.bfloat16)
        self.back.start(((1, 0), (-1, 0), (0, 1), (0, -1)))
        self.back.sib_pass(0, 0)

    def finish(self):
        for dy in range(4):
            for dz in range(4):
                self.back.sib_copy(1 - self.c, dy, dz).wait_recv()
        for cp in self.sent: cp.wait_send()
        self.back.finish()


def sum_scratch(starts):
    V, bf = pltpu.VMEM, jnp.bfloat16
    w = [starts[n + 1] - starts[n] for n in range(4)]
    a, b = w[0] + w[1], w[2] + w[3]
    D = pltpu.SemaphoreType.DMA
    return ([V((4, 4, 48, a + b), bf)] * 2 + [V((4, 48, n), bf) for n in w] + [V((2, 4, 48, a), bf), V((2, 4, 48, b), bf)]
            + [V((48, n), bf) for n in w] + [V((2, 48, a), bf), V((2, 48, b), bf), V((4, 48, 128), bf)]
            + [D((20,)), D((20,)), D((64,)), D((4, 4, 4)), D((4, 4)), D((4, 4))])


OUTPUT_PARTS = (0, 128, 256, 384, 512)
INPUT_PARTS = (0, 256, 384, 512, 640)


def attention_back_kernel(branch, rows, group, cosine, sine, bias, q, k, v, mixed, logsum, extras, wq, wk, wv, wo, o_out, i_out, n_out,
                          grad, probs, back, turned_t, q_back, k_back, v_back, k_acc, v_acc, gsend, grecv):
    f32, low = jnp.float32, jnp.bfloat16
    x = lax.axis_index("tensor")
    def xi(d): return (x + d) % 4
    def xpeer(o):
        return {"tensor": xi(o)}
    barrier = pltpu.get_barrier_semaphore()
    for o in (1, -1):
        pl.semaphore_signal(barrier, inc=1, device_id=xpeer(o), device_id_type=MESH)
    pl.semaphore_wait(barrier, 2)
    sent = []
    def go(cps):
        for cp in cps: cp.start()
        sent.extend(cps)
        return cps
    def ring(n, block, part, to, own):
        there = grad.at[block, pl.ds(64 * part, 64)]
        return pltpu.make_async_remote_copy(
            src_ref=branch.at[pl.ds(64 * part, 64)] if own else there, dst_ref=there,
            send_sem=gsend.at[n], recv_sem=grecv.at[n], device_id=xpeer(to), device_id_type=MESH)
    go([ring(0, x, 0, 1, True), ring(2, x, 1, -1, True)])
    go([ring(1, x, 1, 1, True), ring(3, x, 0, -1, True)])
    grad[x] = branch[...]
    k_t = k[...].astype(f32).T.astype(low)
    logsum_t = logsum[...].T
    bias_t = bias[...].T
    def heads(h):
        one = slice(64 * h, 64 * h + 64)
        kv = slice(64 * (h // 3), 64 * (h // 3) + 64)
        s = lax.dot_general(k[:, kv], q[:, one], NT, preferred_element_type=f32) + bias_t
        probs[h] = jnp.exp(s - logsum_t[h : h + 1, :])
    for h in range(2): heads(h)
    ring(0, xi(-1), 0, 1, False).wait_recv()
    go([ring(4, xi(-1), 0, 1, False)])
    ring(2, xi(1), 1, -1, False).wait_recv()
    go([ring(5, xi(1), 1, -1, False)])
    for h in range(2, 6): heads(h)
    ring(1, xi(-1), 1, 1, False).wait_recv()
    ring(3, xi(1), 0, -1, False).wait_recv()
    ring(4, xi(2), 0, 1, False).wait_recv()
    ring(5, xi(2), 1, -1, False).wait_recv()

    all_grad = grad[...].reshape(512, 1536)
    o_out[:, 0:384] = lax.dot_general(all_grad, mixed[...], TN, preferred_element_type=f32).astype(low)
    back[...] = lax.dot_general(all_grad, wo[...], NT, preferred_element_type=f32).astype(low)
    for h in range(6):
        one = slice(64 * h, 64 * h + 64)
        kv = slice(64 * (h // 3), 64 * (h // 3) + 64)
        p = probs[h]
        grad_p = lax.dot_general(v[:, kv], back[:, one], NT, preferred_element_type=f32)
        both = p * grad_p
        inner = jnp.sum(both, 0, keepdims=True)
        grad_s = (both - p * inner).astype(low)
        v_part = jnp.dot(p.astype(low), back[:, one], preferred_element_type=f32)
        k_part = jnp.dot(grad_s, q[:, one], preferred_element_type=f32)
        if h % 3 == 0:
            v_acc[:, kv] = v_part
            k_acc[:, kv] = k_part
        else:
            v_acc[:, kv] += v_part
            k_acc[:, kv] += k_part
        turned_t[one, :] = jnp.dot(k_t[kv, :], grad_s, preferred_element_type=f32)
    cos, sin = cosine[...], -sine[...]
    q_back[...] = turn(turned_t[...].T * 0.125, cos, sin).astype(low)
    k_back[...] = turn(k_acc[...], cos, sin).astype(low)
    v_back[...] = v_acc[...].astype(low)
    part = (
        lax.dot_general(q_back[...], wq[...], NT, preferred_element_type=f32)
        + lax.dot_general(k_back[...], wk[...], NT, preferred_element_type=f32)
        + lax.dot_general(v_back[...], wv[...], NT, preferred_element_type=f32)
    )
    n_out[...] = part.astype(low)
    t = group[...].astype(f32)
    t = t * lax.rsqrt(jnp.mean(t * t, -1, keepdims=True) + epsilon)
    ones = jnp.ones((512, 128), low)
    gain_part = lax.dot_general((part * t).astype(low), ones, TN, preferred_element_type=f32)
    lane = lax.broadcasted_iota(jnp.int32, (1536, 128), 1)
    o_out[:, 384:512] = jnp.where(lane == 40, gain_part, extras[...]).astype(low)
    i_out[:, 0:384] = lax.dot_general(rows[...], q_back[...], TN, preferred_element_type=f32).astype(low)
    i_out[:, 384:512] = lax.dot_general(rows[...], k_back[...], TN, preferred_element_type=f32).astype(low)
    i_out[:, 512:640] = lax.dot_general(rows[...], v_back[...], TN, preferred_element_type=f32).astype(low)
    for cp in sent: cp.wait_send()


def attention_back(branch, rows, group, cosine, sine, bias, q, k, v, mixed, logsum, extras, wq, wk, wv, wo, cid):
    S = jax.ShapeDtypeStruct
    bf, f32 = jnp.bfloat16, jnp.float32
    V = pltpu.VMEM
    D = pltpu.SemaphoreType.DMA
    return pl.pallas_call(
        attention_back_kernel,
        out_shape=(S((1536, 512), bf), S((1536, 640), bf), S((512, 1536), bf)),
        scratch_shapes=[V((4, 128, 1536), bf), V((6, 512, 512), f32), V((512, 384), bf), V((384, 512), f32), V((512, 384), bf),
                        V((512, 128), bf), V((512, 128), bf), V((512, 128), f32), V((512, 128), f32), D((6,)), D((6,))],
        compiler_params=pltpu.CompilerParams(collective_id=cid, has_side_effects=True, vmem_limit_bytes=60 << 20),
        name="attention_back",
    )(branch, rows, group, cosine, sine, bias, q, k, v, mixed, logsum, extras, wq, wk, wv, wo)


def grad_sum_kernel(o_sum, i_sum, n_part, o_out, i_out, n_out, nr1, nb, nr2, nsend, nrecv, *scratch):
    f32, low = jnp.float32, jnp.bfloat16
    x = lax.axis_index("tensor"); e = lax.axis_index("expert"); y = lax.axis_index("dp")
    z = e // 2; c = e % 2
    def zi(d): return (z + d) % 4
    def yi(d): return (y + d) % 4
    def xi(d): return (x + d) % 4
    def peer(oz, oy):
        return {"expert": zi(oz) * 2 + c, "dp": yi(oy)}
    def xpeer(o):
        return {"tensor": xi(o)}
    partner = {"expert": z * 2 + 1 - c}
    barrier = pltpu.get_barrier_semaphore()
    near = [peer(1, 0), peer(-1, 0), peer(0, 1), peer(0, -1), partner, xpeer(1), xpeer(2), xpeer(3)]
    for p in near:
        pl.semaphore_signal(barrier, inc=1, device_id=p, device_id_type=MESH)
    pl.semaphore_wait(barrier, len(near))
    sent = []
    def go(cps):
        for cp in cps: cp.start()
        sent.extend(cps)
        return cps
    place = (z, y, c, zi, yi, peer, xpeer, partner)
    half = len(scratch) // 2
    osum = TorusSum(o_sum, o_out, scratch[:15], scratch[15:half], OUTPUT_PARTS, place, True)
    isum = TorusSum(i_sum, i_out, scratch[half : half + 15], scratch[half + 15 :], INPUT_PARTS, place, False)
    osum.stage1()
    def nrc(n, src, dst, to):
        return pltpu.make_async_remote_copy(src_ref=src, dst_ref=dst, send_sem=nsend.at[n], recv_sem=nrecv.at[n],
                                            device_id=xpeer(to), device_id_type=MESH)
    n1 = go([nrc(0, n_part.at[xi(2), pl.ds(0, 64)], nr1.at[0], 1), nrc(1, n_part.at[xi(2), pl.ds(64, 64)], nr1.at[1], -1)])
    n2 = go([nrc(2, n_part.at[xi(1), pl.ds(64, 64)], nr2.at[0, pl.ds(64, 64)], 1),
             nrc(3, n_part.at[xi(-1), pl.ds(0, 64)], nr2.at[1, pl.ds(0, 64)], -1)])
    isum.stage1()
    osum.stage2()
    isum.stage2()
    for cp in n1: cp.wait_recv()
    nb[0] = (n_part[xi(1), 0:64].astype(f32) + nr1[0].astype(f32)).astype(low)
    nb[1] = (n_part[xi(-1), 64:128].astype(f32) + nr1[1].astype(f32)).astype(low)
    n3 = go([nrc(4, nb.at[0], nr2.at[0, pl.ds(0, 64)], 1), nrc(5, nb.at[1], nr2.at[1, pl.ds(64, 64)], -1)])
    osum.stage4()
    isum.stage4()
    osum.stage5()
    isum.stage5()
    osum.stage6()
    isum.stage6()
    osum.stage7()
    isum.stage7()
    isum.start_back()
    osum.start_back()
    for cp in n2 + n3: cp.wait_recv()
    n_out[...] = n_part[x].astype(f32) + nr2[0].astype(f32) + nr2[1].astype(f32)
    isum.back.wave1()
    osum.back.wave1()
    isum.back.wave2()
    osum.back.wave2()
    isum.back.wave3()
    osum.back.wave3()
    isum.back.wave4()
    osum.back.wave4()
    isum.finish()
    osum.finish()
    for cp in sent: cp.wait_send()


def grad_sum(o_part, i_part, n_part, cid):
    S = jax.ShapeDtypeStruct
    bf, f32 = jnp.bfloat16, jnp.float32
    V = pltpu.VMEM
    D = pltpu.SemaphoreType.DMA
    vm = pl.BlockSpec(memory_space=pltpu.VMEM)
    o_sums, i_sums, row_sums = pl.pallas_call(
        grad_sum_kernel,
        out_shape=(S((2, 4, 4, 48, 512), bf), S((2, 4, 4, 48, 640), bf), S((128, 1536), f32)),
        in_specs=[vm] * 3,
        out_specs=(vm,) * 3,
        scratch_shapes=[V((2, 64, 1536), bf), V((2, 64, 1536), bf), V((2, 128, 1536), bf),
                        D((6,)), D((6,))] + sum_scratch(OUTPUT_PARTS) + sum_scratch(INPUT_PARTS),
        compiler_params=pltpu.CompilerParams(collective_id=cid, has_side_effects=True, vmem_limit_bytes=40 << 20),
        name="grad_sum",
    )(o_part.reshape(2, 4, 4, 48, 512), i_part.reshape(2, 4, 4, 48, 640), n_part.reshape(4, 128, 1536))
    return o_sums.reshape(1536, 512), i_sums.reshape(1536, 640), row_sums


def attention_tables(documents):
    index = jnp.arange(documents.shape[0], dtype=jnp.int32)
    positions = index - jnp.sum((documents[None, :] < documents[:, None]).astype(jnp.int32), 1)
    freq = 10000.0 ** (-(jnp.arange(32, dtype=jnp.float32) * 2.0 / 64))
    angle = positions.astype(jnp.float32)[:, None] * freq[None, :]
    cos, sin = jnp.cos(angle), jnp.sin(angle)
    allowed = (documents[:, None] == documents[None, :]) & (index[None, :] <= index[:, None])
    return (jnp.concatenate([cos] * 4, 1), jnp.concatenate([-sin, sin] * 2, 1), jnp.where(allowed, 0.0, -1e30).astype(jnp.float32))


def finish_kernel(sums, o_sums, i_sums, gate, up, down, query, key, value, output, router, first, second):
    f32 = jnp.float32
    for n in range(5):
        for i, ref in enumerate((gate, up)):
            ref[n] = sums[:, 0, :, pl.ds(640 * i + 128 * n, 128)].astype(f32).reshape(256, 128)
        down[n] = sums[:, 0, :, pl.ds(1280 + 128 * n, 128)].astype(f32).reshape(256, 128).T
    query[...] = i_sums[:, 0:384].astype(f32)
    key[...] = i_sums[:, 384:512].astype(f32)
    value[...] = i_sums[:, 512:640].astype(f32)
    output[...] = o_sums[:, 0:384].astype(f32).T
    small = o_sums[:, 384:512].astype(f32).T
    router[...] = small[0:40, :]
    first[...] = small[40:41, :]
    second[...] = small[41:42, :]


def finish(sums, o_sums, i_sums):
    S = jax.ShapeDtypeStruct
    f32 = jnp.float32
    return pl.pallas_call(
        finish_kernel,
        grid=(6,),
        out_shape=(S((5, 1536, 128), f32), S((5, 1536, 128), f32), S((5, 128, 1536), f32), S((1536, 384), f32),
                   S((1536, 128), f32), S((1536, 128), f32), S((384, 1536), f32), S((40, 1536), f32), S((1, 1536), f32), S((1, 1536), f32)),
        in_specs=[pl.BlockSpec((4, 1, 64, 1920), lambda j: (0, j, 0, 0)), pl.BlockSpec((256, 512), lambda j: (j, 0)), pl.BlockSpec((256, 640), lambda j: (j, 0))],
        out_specs=(pl.BlockSpec((5, 256, 128), lambda j: (0, j, 0)), pl.BlockSpec((5, 256, 128), lambda j: (0, j, 0)),
                   pl.BlockSpec((5, 128, 256), lambda j: (0, 0, j)), pl.BlockSpec((256, 384), lambda j: (j, 0)),
                   pl.BlockSpec((256, 128), lambda j: (j, 0)), pl.BlockSpec((256, 128), lambda j: (j, 0)),
                   pl.BlockSpec((384, 256), lambda j: (0, j)), pl.BlockSpec((40, 256), lambda j: (0, j)),
                   pl.BlockSpec((1, 256), lambda j: (0, j)), pl.BlockSpec((1, 256), lambda j: (0, j))),
        compiler_params=pltpu.CompilerParams(vmem_limit_bytes=32 << 20),
        name="finish",
    )(sums, o_sums, i_sums)


def expert_back_kernel(acts_hbm, x_hbm, u_hbm, gate_hbm, up_hbm, router_hbm, down_hbm, out, dw_out, router_out,
                       w_ref, down_ref, acts, stage, q, sib, a3, b3, a4, b4, a5, b5, a6, b6, xu, acc, dwb, ya, yb,
                       w_sem, down_sem, act_sem, load_sem, sib_send, sib_recv, ssem, rsem, ysend, yrecv):
    f32, low = jnp.float32, jnp.bfloat16
    nk = 12
    wide = 640
    x = lax.axis_index("tensor"); e = lax.axis_index("expert"); y = lax.axis_index("dp")
    z = e // 2; c = e % 2
    def zi(d): return (z + d) % 4
    def xi(d): return (x + d) % 4
    def yi(d): return (y + d) % 4
    def peer(oz, ox):
        return {"expert": zi(oz) * 2 + c, "tensor": xi(ox)}
    def ypeer(o):
        return {"dp": yi(o)}
    partner = {"expert": z * 2 + 1 - c}

    def act_load(n):
        return pltpu.make_async_copy(acts_hbm.at[:, :, n], acts.at[:, :, n], act_sem.at[n])
    def x_load(j, k):
        cols = pl.ds(pl.multiple_of(j * 256, 256), 256)
        return [pltpu.make_async_copy(x_hbm.at[:, :, :, :, cols], xu.at[k % 2], load_sem.at[k % 2, 0])]
    def u_load(j, k):
        cols = pl.ds(pl.multiple_of(j * 256, 256), 256)
        return [pltpu.make_async_copy(u_hbm.at[:, :, :, :, cols], xu.at[k % 2], load_sem.at[k % 2, 1])]
    w_loads = weight_loads(gate_hbm, up_hbm, router_hbm, w_ref, w_sem)
    down_load = pltpu.make_async_copy(down_hbm, down_ref, down_sem)
    down_load.start()
    act_load(1 - c).start()
    act_load(c).start()
    for cp in x_load(0, 0): cp.start()
    for cp in w_loads: cp.start()
    barrier = pltpu.get_barrier_semaphore()
    near = [peer(1, 0), peer(-1, 0), peer(0, 1), peer(0, -1), partner, ypeer(1), ypeer(-1)]
    for p in near:
        pl.semaphore_signal(barrier, inc=1, device_id=p, device_id_type=MESH)
    pl.semaphore_wait(barrier, len(near))

    def sibs(k):
        return [pltpu.make_async_remote_copy(
            src_ref=stage.at[k % 2], dst_ref=sib.at[k % 2],
            send_sem=sib_send.at[k], recv_sem=sib_recv.at[k], device_id=partner, device_id_type=MESH)]
    def rc(k, n, src, dst, to):
        return pltpu.make_async_remote_copy(src_ref=src, dst_ref=dst, send_sem=ssem.at[k, n], recv_sem=rsem.at[k, n],
                                            device_id=to, device_id_type=MESH)
    def copies3(k):
        s = k % 4
        return [rc(k, 0, q.at[k % 9, zi(2), :, pl.ds(0, 32)], a3.at[s, 0], peer(1, 0)),
                rc(k, 1, q.at[k % 9, zi(2), :, pl.ds(32, 32)], a3.at[s, 1], peer(-1, 0)),
                rc(k, 2, q.at[k % 9, :, xi(2), pl.ds(64, 32)], b3.at[s, 0], peer(0, 1)),
                rc(k, 3, q.at[k % 9, :, xi(2), pl.ds(96, 32)], b3.at[s, 1], peer(0, -1))]
    def copies4(k):
        s = k % 4
        return [rc(k, 4, q.at[k % 9, zi(1), :, pl.ds(0, 64)], a4.at[s, 0], peer(1, 0)),
                rc(k, 5, q.at[k % 9, zi(-1), :, pl.ds(0, 64)], a4.at[s, 1], peer(-1, 0)),
                rc(k, 6, q.at[k % 9, :, xi(1), pl.ds(64, 64)], b4.at[s, 0], peer(0, 1)),
                rc(k, 7, q.at[k % 9, :, xi(-1), pl.ds(64, 64)], b4.at[s, 1], peer(0, -1))]
    def copies5(k):
        s = k % 4
        return [rc(k, 8, q.at[k % 9, z, xi(2), pl.ds(0, 32)], a5.at[s, 0], peer(0, 1)),
                rc(k, 9, q.at[k % 9, z, xi(2), pl.ds(32, 32)], a5.at[s, 1], peer(0, -1)),
                rc(k, 10, q.at[k % 9, zi(2), x, pl.ds(64, 32)], b5.at[s, 0], peer(1, 0)),
                rc(k, 11, q.at[k % 9, zi(2), x, pl.ds(96, 32)], b5.at[s, 1], peer(-1, 0))]
    def copies6(k):
        s = k % 4
        return [rc(k, 12, q.at[k % 9, z, xi(1), pl.ds(0, 64)], a6.at[s, 0], peer(0, 1)),
                rc(k, 13, q.at[k % 9, z, xi(-1), pl.ds(0, 64)], a6.at[s, 1], peer(0, -1)),
                rc(k, 14, q.at[k % 9, zi(1), x, pl.ds(64, 64)], b6.at[s, 0], peer(1, 0)),
                rc(k, 15, q.at[k % 9, zi(-1), x, pl.ds(64, 64)], b6.at[s, 1], peer(-1, 0))]
    def add(k, i, j, rows, *terms):
        t = q[k % 9, i, j, rows].astype(f32)
        for s in terms:
            t = t + s.astype(f32)
        q[k % 9, i, j, rows] = t.astype(low)

    def product(k, cc, put):
        cols = pl.ds(pl.multiple_of((k // 2) * 256, 256), 256)
        def rows(lanes): return acts[:, :, cc, :, lanes].reshape(2048, -1)
        @pl.when(k % 2 == 0)
        def _():
            put(jnp.dot(rows(slice(0, wide)), down_ref[:, cols], preferred_element_type=f32))
        @pl.when(k % 2 == 1)
        def _():
            put(lax.dot_general(rows(slice(wide, 2048)), w_ref[cols, :], (((1,), (1,)), ((), ())),
                                preferred_element_type=f32))

    def stage1(k):
        @pl.when(k == 0)
        def _():
            down_load.wait()
            act_load(1 - c).wait()
        @pl.when(k == 1)
        def _():
            for cp in w_loads: cp.wait()
        def put(r):
            stage[k % 2] = r.astype(low).reshape(4, 4, 128, 256)
        product(k, 1 - c, put)
        for cp in sibs(k): cp.start()

    def stage2(k):
        for cp in sibs(k): cp.wait()
        def put(r):
            q[k % 9] = (r.reshape(4, 4, 128, 256) + sib[k % 2].astype(f32)).astype(low)
        product(k, c, put)
        for cp in copies3(k): cp.start()

    def weight_part(k):
        @pl.when(k == 0)
        def _(): act_load(c).wait()
        @pl.when(k % 2 == 0)
        def _():
            for cp in x_load(0, k): cp.wait()
            for cp in u_load(k // 2, k + 1): cp.start()
        @pl.when(k % 2 == 1)
        def _():
            for cp in u_load(0, k): cp.wait()
        @pl.when((k + 1 < nk) & (k % 2 == 1))
        def _():
            for cp in x_load(k // 2 + 1, k + 1): cp.start()
        slot = (k // 2) % 3
        def make(lanes):
            return lax.dot_general(xu[k % 2].reshape(4096, 256), acts[:, :, :, :, lanes].reshape(4096, -1),
                                   (((0,), (0,)), ((), ())), preferred_element_type=f32)
        @pl.when(k % 2 == 0)
        def _():
            acc[...] = make(slice(wide, 2048))
            dwb[slot, :, :, 0 : 2 * wide] = acc[:, 0 : 2 * wide].astype(low).reshape(4, 64, 2 * wide)
            router_out[pl.ds(pl.multiple_of((k // 2) * 256, 256), 256), :] = acc[:, 2 * wide :]
        @pl.when(k % 2 == 1)
        def _():
            acc[:, 0:wide] = make(slice(0, wide))
            dwb[slot, :, :, 2 * wide :] = acc[:, 0:wide].astype(low).reshape(4, 64, wide)

    def yrc(j, n, src, dst, to):
        return pltpu.make_async_remote_copy(src_ref=src, dst_ref=dst, send_sem=ysend.at[j, n], recv_sem=yrecv.at[j, n],
                                            device_id=to, device_id_type=MESH)
    def ycopies1(j):
        s = j % 3
        return [yrc(j, 0, dwb.at[s, yi(2), pl.ds(0, 32)], ya.at[j % 4, 0], ypeer(1)),
                yrc(j, 1, dwb.at[s, yi(2), pl.ds(32, 32)], ya.at[j % 4, 1], ypeer(-1))]
    def ycopies2(j):
        s = j % 3
        return [yrc(j, 2, dwb.at[s, yi(1)], yb.at[j % 4, 0], ypeer(1)),
                yrc(j, 3, dwb.at[s, yi(-1)], yb.at[j % 4, 1], ypeer(-1))]
    def ystage1(j):
        for cp in ycopies1(j): cp.start()
    def ystage2(j):
        for cp in ycopies1(j): cp.wait_recv()
        s = j % 3
        for d, r, m in ((1, 0, 0), (-1, 32, 1)):
            dwb[s, yi(d), pl.ds(r, 32)] = (dwb[s, yi(d), pl.ds(r, 32)].astype(f32) + ya[j % 4, m].astype(f32)).astype(low)
        for cp in ycopies2(j): cp.start()
    def ystage3(j):
        for cp in ycopies2(j): cp.wait_recv()
        dw_out[j] = (dwb[j % 3, y].astype(f32) + yb[j % 4, 0].astype(f32) + yb[j % 4, 1].astype(f32)).astype(low)
        for cp in ycopies1(j) + ycopies2(j): cp.wait_send()

    def stage4(k):
        for cp in copies3(k): cp.wait_recv()
        s = k % 4
        def body(n, _):
            add(k, zi(1), n, pl.ds(0, 32), a3[s, 0, n])
            add(k, zi(-1), n, pl.ds(32, 32), a3[s, 1, n])
            add(k, n, xi(1), pl.ds(64, 32), b3[s, 0, n])
            add(k, n, xi(-1), pl.ds(96, 32), b3[s, 1, n])
            return 0
        lax.fori_loop(0, 4, body, 0)
        for cp in copies4(k): cp.start()
    def stage5(k):
        for cp in copies4(k): cp.wait_recv()
        s = k % 4
        def body(n, _):
            add(k, z, n, pl.ds(0, 64), a4[s, 0, n], a4[s, 1, n])
            add(k, n, x, pl.ds(64, 64), b4[s, 0, n], b4[s, 1, n])
            return 0
        lax.fori_loop(0, 4, body, 0)
        for cp in copies5(k): cp.start()
    def stage6(k):
        for cp in copies5(k): cp.wait_recv()
        s = k % 4
        add(k, z, xi(1), pl.ds(0, 32), a5[s, 0])
        add(k, z, xi(-1), pl.ds(32, 32), a5[s, 1])
        add(k, zi(1), x, pl.ds(64, 32), b5[s, 0])
        add(k, zi(-1), x, pl.ds(96, 32), b5[s, 1])
        for cp in copies6(k): cp.start()
    def stage7(k):
        for cp in copies6(k): cp.wait_recv()
        s = k % 4
        for h, m in ((0, a6), (64, b6)):
            t = q[k % 9, z, x, pl.ds(h, 64)].astype(f32) + m[s, 0].astype(f32) + m[s, 1].astype(f32)
            out[k % 2, pl.ds(h, 64), pl.ds(pl.multiple_of((k // 2) * 256, 256), 256)] = t
        for cp in copies3(k) + copies4(k) + copies5(k) + copies6(k): cp.wait_send()

    def step(i, _):
        for lag, st in ((8, stage7), (7, stage6), (5, stage5), (3, stage4), (1, stage2), (0, stage1)):
            k = i - lag
            @pl.when((k >= 0) & (k < nk))
            def _():
                st(k)
        n = i - 0
        for lag, st in ((5, ystage3), (3, ystage2)):
            k = n - lag
            @pl.when((k >= 0) & (k < nk) & (k % 2 == 0))
            def _():
                st(k // 2)
        @pl.when((n >= 0) & (n < nk))
        def _():
            weight_part(n)
            @pl.when(n % 2 == 1)
            def _():
                ystage1(n // 2)
        return 0
    lax.fori_loop(0, nk + 8, step, 0)


def expert_back(acts, x, u, gate, up, router, down, cid):
    bf = jnp.bfloat16
    V = pltpu.VMEM
    nk = 12
    D = pltpu.SemaphoreType.DMA
    vm = pl.BlockSpec(memory_space=pltpu.VMEM)
    anym = pl.BlockSpec(memory_space=pl.ANY)
    return pl.pallas_call(
        expert_back_kernel,
        out_shape=(jax.ShapeDtypeStruct((2, 128, 1536), jnp.float32),
                   jax.ShapeDtypeStruct((6, 64, 1920), bf),
                   jax.ShapeDtypeStruct((1536, 128), jnp.float32)),
        in_specs=[anym] * 7,
        out_specs=(vm, vm, vm),
        scratch_shapes=[V((1536, 1408), bf), V((640, 1536), bf), V((4, 4, 2, 128, 2048), bf), V((2, 4, 4, 128, 256), bf), V((9, 4, 4, 128, 256), bf), V((2, 4, 4, 128, 256), bf),
                        V((4, 2, 4, 32, 256), bf), V((4, 2, 4, 32, 256), bf),
                        V((4, 2, 4, 64, 256), bf), V((4, 2, 4, 64, 256), bf),
                        V((4, 2, 32, 256), bf), V((4, 2, 32, 256), bf),
                        V((4, 2, 64, 256), bf), V((4, 2, 64, 256), bf),
                        V((2, 4, 4, 2, 128, 256), bf), V((256, 1408), jnp.float32), V((3, 4, 64, 1920), bf),
                        V((4, 2, 32, 1920), bf), V((4, 2, 64, 1920), bf),
                        D((11,)), D(()), D((2,)), D((2, 2)), D((nk,)), D((nk,)), D((nk, 16)), D((nk, 16)), D((6, 4)), D((6, 4))],
        compiler_params=pltpu.CompilerParams(collective_id=cid, has_side_effects=True, vmem_limit_bytes=63 << 20),
        name="expert_back",
    )(acts, x, u, gate, up, router, down)


def shards(
    tokens,
    documents,
    expert_routes,
    attention_gain,
    query_weight,
    key_matrix,
    value_matrix,
    output_weight,
    expert_gain,
    router_weight,
    gate_weight,
    up_weight,
    down_weight,
    out_cotangent,
):
    width = tokens.shape[1]
    local_experts = gate_weight.shape[0]
    experts_all = router_weight.shape[1]
    wide = local_experts * gate_weight.shape[2]
    inputs = tokens.astype(jnp.float32)
    first_gain = attention_gain.astype(jnp.float32)
    second_gain = expert_gain.astype(jnp.float32)
    first_scale = lax.rsqrt(jnp.mean(inputs * inputs, -1, keepdims=True) + epsilon)
    tables = attention_tables(documents)
    attention_weights = (query_weight, key_matrix, value_matrix, output_weight)
    router_pad = jnp.pad(router_weight, ((0, 0), (0, 64 - experts_all)))
    expert_weights = (
        gate_weight,
        up_weight,
        jnp.concatenate([router_pad, router_pad], 1),
        down_weight.reshape(wide, width),
    )
    lined_routes = jnp.pad(expert_routes, ((0, 0), (0, 128 - expert_routes.shape[1])))
    (
        residual,
        plane_rows,
        acts,
        plane_upstream,
        group_tokens,
        group_rows,
        queries,
        keys,
        values,
        attended,
        logsum,
    ) = front(
        tokens,
        jnp.concatenate([out_cotangent, lined_routes.astype(jnp.bfloat16)], 1),
        first_gain.reshape(1, width),
        second_gain.reshape(1, width),
        *tables,
        *attention_weights,
        *expert_weights,
        6,
    )
    experts_index = jnp.arange(experts_all, dtype=jnp.int32)
    second_normed, second_scale = normalize(residual, second_gain)
    second_low = second_normed.astype(jnp.bfloat16)
    def dense_gates(rows, routes):
        named = jnp.any(routes[:, :, None] == experts_index[None, None, :], 1)
        logits = jnp.dot(rows, router_weight, preferred_element_type=jnp.float32)
        logits = jnp.where(named, logits, -1e30)
        raised = jnp.exp(logits - jnp.max(logits, -1, keepdims=True))
        return raised / jnp.sum(raised, -1, keepdims=True)

    sums, weight_grads, router_pairs = expert_back(
        acts, plane_rows, plane_upstream, *expert_weights, 2
    )
    mixture, route_rows = sums[0], sums[1]
    layer_output = (residual + mixture).astype(jnp.bfloat16)
    router_pairs = router_pairs[:, :experts_all] + router_pairs[:, 64 : 64 + experts_all]
    weight_grads = lax.all_gather(weight_grads, "dp", axis=0)
    gates = dense_gates(second_low, expert_routes)
    upstream = out_cotangent.astype(jnp.float32)
    shared = gates * jnp.sum(mixture * upstream, -1, keepdims=True)
    router_local = -jnp.einsum(
        "td,te->de",
        second_low.astype(jnp.float32),
        shared,
        precision=highest,
        preferred_element_type=jnp.float32,
    ) + router_pairs
    normed_back = route_rows - jnp.einsum(
        "te,de->td",
        shared,
        router_weight.astype(jnp.float32),
        precision=highest,
        preferred_element_type=jnp.float32,
    )
    residual_back, expert_gain_local = norm_back(residual, second_scale, second_gain, normed_back)
    residual_grad = upstream + residual_back
    small = jnp.concatenate(
        [
            router_local,
            jnp.zeros((width, 1), jnp.float32),
            expert_gain_local[:, None],
            jnp.zeros((width, 126 - experts_all), jnp.float32),
        ],
        1,
    )
    output_part, input_part, normed_part = attention_back(
        residual_grad.astype(jnp.bfloat16),
        group_rows,
        group_tokens.reshape(-1, width),
        *tables,
        queries,
        keys,
        values,
        attended,
        logsum,
        small,
        *attention_weights,
        7,
    )
    output_sums, input_sums, normed_grad = grad_sum(output_part, input_part, normed_part, 4)
    input_back, _ = norm_back(inputs, first_scale, first_gain, normed_grad)
    input_gradient = residual_grad + input_back
    (
        gate_gradient,
        up_gradient,
        down_gradient,
        query_gradient,
        key_gradient,
        value_gradient,
        output_gradient,
        router_gradient,
        attention_gain_gradient,
        expert_gain_gradient,
    ) = finish(weight_grads, output_sums, input_sums)
    router_gradient = router_gradient.T
    attention_gain_gradient = attention_gain_gradient.reshape(width)
    expert_gain_gradient = expert_gain_gradient.reshape(width)
    return (
        layer_output,
        input_gradient,
        attention_gain_gradient,
        query_gradient,
        key_gradient,
        value_gradient,
        output_gradient,
        expert_gain_gradient,
        router_gradient,
        gate_gradient,
        up_gradient,
        down_gradient,
    )


def solution(mesh):
    placed = (
        P(("dp", "expert", "tensor"), None),
        P(("dp", "expert")),
        P(("dp", "expert", "tensor"), None),
        P(),
        P(None, "tensor"),
        P(None, "tensor"),
        P(None, "tensor"),
        P("tensor", None),
        P(),
        P(),
        P("expert", None, "tensor"),
        P("expert", None, "tensor"),
        P("expert", "tensor", None),
        P(("dp", "expert", "tensor"), None),
    )
    return jax.shard_map(
        shards,
        mesh=mesh,
        in_specs=placed,
        out_specs=(
            P(("dp", "expert", "tensor"), None),
            P(("dp", "expert", "tensor"), None),
            P(),
            P(None, "tensor"),
            P(None, "tensor"),
            P(None, "tensor"),
            P("tensor", None),
            P(),
            P(),
            P("expert", None, "tensor"),
            P("expert", None, "tensor"),
            P("expert", "tensor", None),
        ),
        check_vma=False,
    )
```

profile of v0, /device:TPU:1, one launch (start us, length us, event | category | flops | bytes accessed | tf_op | source)
XLA Modules:
  0.0 367.2 jit_solution(5530235143145329808)
XLA Ops:
  7.2 0.0 copy-start.13
  7.2 0.0 copy-start.12
  7.2 0.0 copy-start.11
  7.2 0.0 all-gather.3.cloned.1.call-start
  7.3 1.0 convert_reduce_fusion
  8.3 0.0 copy-start.6
  8.3 1.9 fusion.2.bias
  10.2 1.1 copy.46
  11.3 0.1 pad.10
  11.4 1.0 pad_maximum_fusion.router_hbm
  12.4 0.0 copy-done.13
  12.4 0.1 copy.44
  12.5 0.0 copy-done.12
  12.5 0.6 reshape.114.first_gain
  13.1 0.0 copy-done.11
  13.1 0.6 reshape.115.second_gain
  13.7 1.0 fusion.13
  14.7 0.0 copy-done.6
  14.7 0.8 fusion.11.u_own
  15.5 1.3 pad_maximum_fusion.1
  16.8 123.2 %front.1 = (f32[128,1536]{1,0:T(8,128)}, bf16[4,4,2,128,1536]{4,3,2,1,0:T(8,128)(2,1)}, bf16[4,4,2,128,2048]{4,3,2,1,0:T(8,128)(2,1)}, bf16[4,4,2,128,1664]{4,3,...) custom-call(bf16[128,1536]{1,0:T(8,128)(2,1)} %tokens.1, ...), custom_call_target="tpu_custom_call" | custom-call | tf_op jit(solution)/shard_map/front/pallas_call | solution.py:370
  140.0 110.6 %expert_back.1 = (f32[2,128,1536]{2,1,0:T(8,128)}, bf16[6,64,1920]{2,1,0:T(8,128)(2,1)}, f32[1536,128]{1,0:T(8,128)}) custom-call(bf16[4,4,2,128,2048]{4,3,2,1,0:T(8,128)(2,1)} %get-tuple-element.43.acts_hbm, bf16[4,4,2,128,1536]{4,3,2,1,0:T(8,128)(2,1)} %get-tuple-element.44.x_hbm, bf16[4,4,2,128,1664]{4,3,2,1,0:T(8,128)(2,1)} %get-tuple-element.45.u_hbm, ...), custom_call_target="tpu_custom_call" | custom-call | tf_op jit(solution)/shard_map/expert_back/pallas_call | solution.py:977
  250.5 0.0 copy-start.4
  250.5 0.0 copy-start.9
  250.6 0.0 all-gather.3.cloned.1.call-update
  250.6 0.0 copy-start.8
  250.6 1.0 copy-done.4
  251.7 2.0 fusion.4
  253.7 0.0 copy-done.9
  253.7 0.0 copy-start.10
  253.7 0.3 fusion.16
  254.1 0.0 copy-done.8
  254.1 0.8 multiply_reduce_fusion
  254.9 0.3 broadcast_in_dim.24
  255.1 0.1 pad.14.clone
  255.2 0.1 pad.12.clone
  255.3 0.0 copy-done.10
  255.3 0.7 fusion
  256.0 1.2 maximum_maximum_fusion.extras
  257.1 1.3 fusion.15
  258.4 29.1 %attention_back.1 = (bf16[1536,512]{1,0:T(8,128)(2,1)}, bf16[1536,640]{1,0:T(8,128)(2,1)}, bf16[512,1536]{1,0:T(8,128)(2,1)}) custom-call(bf16[128,1536]{1,0:T(8,128)(2,1)} %get-tuple-element.76.branch, bf16[512,1536]{1,0:T(8,128)(2,1)} %get-tuple-element.47.rows, bf16[512,1536]{1,0:T(8,128)(2,1)} %bitcast.27, f32[512,128]{1,0:T(8,128)} %get-tuple-element.91.cosine, ...), custom_call_target="tpu_custom_call" | custom-call | tf_op jit(solution)/shard_map/attention_back/pallas_call | solution.py:616
  287.5 0.0 copy-start.1
  287.5 1.6 copy-done.1
  289.1 0.0 copy-start.2
  289.1 1.4 copy-done.2
  290.5 0.0 copy-start.3
  290.5 1.4 copy-done.3
  291.9 0.0 copy-start.5
  291.9 0.0 copy-start.7
  291.9 55.8 %grad_sum.1 = (bf16[2,4,4,48,512]{4,3,2,1,0:T(8,128)(2,1)S(1)}, bf16[2,4,4,48,640]{4,3,2,1,0:T(8,128)(2,1)S(1)}, f32[128,1536]{1,0:T(8,128)S(1)}) custom-call(bf16[2,4,4,48,512]{4,3,2,1,0:T(8,128)(2,1)S(1)} %bitcast.23, bf16[2,4,4,48,640]{4,3,2,1,0:T(8,128)(2,1)S(1)} %bitcast.21, bf16[4,128,1536]{2,1,0:T(8,128)(2,1)S(1)} %bitcast.24), custom_call_target="tpu_custom_call" | custom-call | tf_op jit(solution)/shard_map/grad_sum/pallas_call | solution.py:697
  347.8 0.0 copy-done.5
  347.8 0.2 fusion.5
  348.1 0.0 copy-done.7
  348.1 1.2 fusion.8
  349.3 0.0 all-gather.3.cloned.1.call-done
  349.3 0.0 copy-start
  349.3 2.7 copy-done
  352.0 6.7 %finish.1 = (f32[5,1536,128]{2,1,0:T(8,128)}, f32[5,1536,128]{2,1,0:T(8,128)}, f32[5,128,1536]{2,1,0:T(8,128)}, f32[1536,384]{1,0:T(8,128)}, f32[1536,128]{1,0:T...) custom-call(bf16[4,6,64,1920]{3,2,1,0:T(8,128)(2,1)S(1)} %bitcast.19, ...), custom_call_target="tpu_custom_call" | custom-call | tf_op jit(solution)/shard_map/finish/pallas_call | solution.py:739
  358.7 0.6 reduce
  359.3 0.6 reduce.1
  (12 shorter events, 0.1 us)
Async XLA Ops:
  7.2 5.2 %copy-start.13 = (s32[128,8]{0,1:T(8,128)S(1)}, s32[128,8]{0,1:T(8,128)}, u32[]{:S(2)}) copy-start(s32[128,8]{0,1:T(8,128)} %param.16) | copy-start | bytes 12292
  7.2 5.3 %copy-start.12 = (bf16[1536]{0:T(1024)(128)(2,1)S(1)}, bf16[1536]{0:T(1024)(128)(2,1)}, u32[]{:S(2)}) copy-start(bf16[1536]{0:T(1024)(128)(2,1)} %param.17) | copy-start | bytes 9220
  7.2 5.9 %copy-start.11 = (bf16[1536]{0:T(1024)(128)(2,1)S(1)}, bf16[1536]{0:T(1024)(128)(2,1)}, u32[]{:S(2)}) copy-start(bf16[1536]{0:T(1024)(128)(2,1)} %param.22) | copy-start | bytes 9220
  7.2 342.1 %all-gather.3.cloned.1.call-start = ((), (), s32[]{:S(2)}) async-start(), calls=%async_computation | async-start | bytes 7372800 | tf_op jit(solution)/shard_map/all_gather | solution.py:1069
  8.3 6.4 %copy-start.6 = (bf16[128,1536]{1,0:T(8,128)(2,1)S(1)}, bf16[128,1536]{1,0:T(8,128)(2,1)}, u32[]{:S(2)}) copy-start(bf16[128,1536]{1,0:T(8,128)(2,1)} %param.27) | copy-start | bytes 1179652
  250.5 1.1 copy-start.4
  250.5 3.2 copy-start.9
  250.6 3.5 copy-start.8
  253.7 1.6 copy-start.10
  287.5 1.6 copy-start.1
  289.1 1.4 copy-start.2
  290.5 1.4 copy-start.3
  291.9 55.8 %copy-start.5 = (bf16[128,1536]{1,0:T(8,128)(2,1)S(1)}, bf16[128,1536]{1,0:T(8,128)(2,1)}, u32[]{:S(2)}) copy-start(bf16[128,1536]{1,0:T(8,128)(2,1)} %tokens.1) | copy-start | bytes 1179652
  291.9 56.1 %copy-start.7 = (f32[128,1536]{1,0:T(8,128)S(1)}, f32[128,1536]{1,0:T(8,128)}, u32[]{:S(2)}) copy-start(f32[128,1536]{1,0:T(8,128)} %get-tuple-element.77) | copy-start | bytes 2359300
  349.3 2.7 copy-start
Sparse Core Ops, SparseCore 0:
  250.7 70.1 all-gather.2
where the time goes:
time: 374 us; the launch traced here: 367 us
  Pallas kernels  325 us (87%)
  between operations  14.7 us (4%)
  other arithmetic  14.2 us (4%)
  local copies, waits for them, and re-layouts  11.1 us (3%)
    pallas_call x1, Pallas kernels, front(): pl.pallas_call(front_kernel, out_shape=(S((n, width), f32), S((4, 4, 2, n...  123 us
    pallas_call x1, Pallas kernels, expert_back(): pl.pallas_call(expert_back_kernel, out_shape=(jax.ShapeDtypeStruct((2, 12...  111 us
    pallas_call x1, Pallas kernels, grad_sum(): pl.pallas_call(grad_sum_kernel, out_shape=(S((2, 4, 4, 48, 512), bf), S((...  55.8 us
    pallas_call x1, Pallas kernels, attention_back(): pl.pallas_call(attention_back_kernel, out_shape=(S((1536, 512), bf), S((1...  29.1 us
    unnamed x29, local copies, waits for them, and re-layouts  9.28 us
  transfers between devices with their start and end apart: 1, of which 0 were waited for; matrix products, arithmetic and copies ran while one was open for 2% of the time, Pallas kernels for 23%

commit v1 on v0

--- a/solution.py
+++ b/solution.py
@@ -9,20 +9,12 @@
 
 
 epsilon = 1e-06
-highest = lax.Precision.HIGHEST
-
-
-def normalize(value_rows, gain):
-    scale = lax.rsqrt(jnp.mean(value_rows * value_rows, -1, keepdims=True) + epsilon)
-    return (value_rows * scale * gain, scale)
 
 
 def norm_back(value_rows, scale, gain, upstream):
     weighted = upstream * gain
     inner = jnp.mean(weighted * value_rows, -1, keepdims=True)
-    result = scale * weighted - value_rows * scale**3 * inner
-    gain_part = jnp.sum(upstream * value_rows * scale, 0)
-    return (result, gain_part)
+    return scale * weighted - value_rows * scale**3 * inner
 
 
 MESH = pl.DeviceIdType.MESH
@@ -523,8 +515,24 @@
 INPUT_PARTS = (0, 256, 384, 512, 640)
 
 
-def attention_back_kernel(branch, rows, group, cosine, sine, bias, q, k, v, mixed, logsum, extras, wq, wk, wv, wo, o_out, i_out, n_out,
-                          grad, probs, back, turned_t, q_back, k_back, v_back, k_acc, v_acc, gsend, grecv):
+BACK_INPUTS = (
+    ((2, 128, 1536), "float32"), ((128, 1536), "float32"), ((128, 1536), "bfloat16"), ((128, 8), "int32"), ((1, 1536), "float32"),
+    ((1536, 128), "bfloat16"), ((1536, 128), "float32"), ((512, 1536), "bfloat16"), ((512, 1536), "bfloat16"), ((512, 128), "float32"),
+    ((512, 128), "float32"), ((512, 512), "float32"), ((512, 384), "bfloat16"), ((512, 128), "bfloat16"), ((512, 128), "bfloat16"),
+    ((512, 384), "bfloat16"), ((512, 128), "float32"), ((1536, 384), "bfloat16"), ((1536, 128), "bfloat16"), ((1536, 128), "bfloat16"),
+    ((384, 1536), "bfloat16"),
+)
+
+
+def attention_back_kernel(*refs):
+    count = len(BACK_INPUTS)
+    given, (residual_grad, o_out, i_out, n_out) = refs[:count], refs[count : count + 4]
+    held = refs[count + 4 : 2 * count + 4]
+    (sums, residual, cotangent, routes, second_gain, router, router_pairs, rows, group, cosine, sine, bias, q, k, v, mixed, logsum,
+     wq, wk, wv, wo) = held
+    (branch, grad, probs, back, turned_t, q_back, k_back, v_back, k_acc, v_acc, gsend, grecv, load_sem) = refs[2 * count + 4 :]
+    loads = [pltpu.make_async_copy(a, b, load_sem.at[n]) for n, (a, b) in enumerate(zip(given, held))]
+    for cp in loads: cp.start()
     f32, low = jnp.float32, jnp.bfloat16
     x = lax.axis_index("tensor")
     def xi(d): return (x + d) % 4
@@ -539,6 +547,27 @@
         for cp in cps: cp.start()
         sent.extend(cps)
         return cps
+    for cp in loads[:6]: cp.wait()
+    res = residual[...]
+    scale = lax.rsqrt(jnp.mean(res * res, -1, keepdims=True) + epsilon)
+    normed = (res * scale * second_gain[...]).astype(low)
+    lane = lax.broadcasted_iota(jnp.int32, (128, 128), 1)
+    named = lane == routes[:, 0:1]
+    for n in range(1, 8):
+        named = named | (lane == routes[:, n : n + 1])
+    logits = jnp.where(named, jnp.dot(normed, router[...], preferred_element_type=f32), -1e30)
+    raised = jnp.exp(logits - jnp.max(logits, -1, keepdims=True))
+    gates = raised / jnp.sum(raised, -1, keepdims=True)
+    upstream = cotangent[...].astype(f32)
+    shared = gates * jnp.sum(sums[0] * upstream, -1, keepdims=True)
+    high = shared.astype(low).astype(f32)
+    shared = jnp.where(lane < 64, high, pltpu.roll(shared - high, 64, 1)).astype(low)
+    normed_back = sums[1] - lax.dot_general(shared, router[...], NT, preferred_element_type=f32)
+    weighted = normed_back * second_gain[...]
+    inner = jnp.mean(weighted * res, -1, keepdims=True)
+    total = upstream + scale * weighted - res * scale**3 * inner
+    residual_grad[...] = total
+    branch[...] = total.astype(low)
     def ring(n, block, part, to, own):
         there = grad.at[block, pl.ds(64 * part, 64)]
         return pltpu.make_async_remote_copy(
@@ -547,6 +576,7 @@
     go([ring(0, x, 0, 1, True), ring(2, x, 1, -1, True)])
     go([ring(1, x, 1, 1, True), ring(3, x, 0, -1, True)])
     grad[x] = branch[...]
+    for cp in loads[6:]: cp.wait()
     k_t = k[...].astype(f32).T.astype(low)
     logsum_t = logsum[...].T
     bias_t = bias[...].T
@@ -556,6 +586,10 @@
         s = lax.dot_general(k[:, kv], q[:, one], NT, preferred_element_type=f32) + bias_t
         probs[h] = jnp.exp(s - logsum_t[h : h + 1, :])
     for h in range(2): heads(h)
+    ones = jnp.ones((128, 128), low)
+    gain_two = lax.dot_general((normed_back * res * scale).astype(low), ones, TN, preferred_element_type=f32)
+    extras = router_pairs[...] - lax.dot_general(normed, shared, TN, preferred_element_type=f32)
+    extras = extras + pltpu.roll(extras, 64, 1)
     ring(0, xi(-1), 0, 1, False).wait_recv()
     go([ring(4, xi(-1), 0, 1, False)])
     ring(2, xi(1), 1, -1, False).wait_recv()
@@ -601,26 +635,30 @@
     ones = jnp.ones((512, 128), low)
     gain_part = lax.dot_general((part * t).astype(low), ones, TN, preferred_element_type=f32)
     lane = lax.broadcasted_iota(jnp.int32, (1536, 128), 1)
-    o_out[:, 384:512] = jnp.where(lane == 40, gain_part, extras[...]).astype(low)
+    o_out[:, 384:512] = jnp.where(lane == 40, gain_part, jnp.where(lane == 41, gain_two, extras)).astype(low)
     i_out[:, 0:384] = lax.dot_general(rows[...], q_back[...], TN, preferred_element_type=f32).astype(low)
     i_out[:, 384:512] = lax.dot_general(rows[...], k_back[...], TN, preferred_element_type=f32).astype(low)
     i_out[:, 512:640] = lax.dot_general(rows[...], v_back[...], TN, preferred_element_type=f32).astype(low)
     for cp in sent: cp.wait_send()
 
 
-def attention_back(branch, rows, group, cosine, sine, bias, q, k, v, mixed, logsum, extras, wq, wk, wv, wo, cid):
+def attention_back(*operands, cid):
     S = jax.ShapeDtypeStruct
     bf, f32 = jnp.bfloat16, jnp.float32
     V = pltpu.VMEM
     D = pltpu.SemaphoreType.DMA
     return pl.pallas_call(
         attention_back_kernel,
-        out_shape=(S((1536, 512), bf), S((1536, 640), bf), S((512, 1536), bf)),
-        scratch_shapes=[V((4, 128, 1536), bf), V((6, 512, 512), f32), V((512, 384), bf), V((384, 512), f32), V((512, 384), bf),
-                        V((512, 128), bf), V((512, 128), bf), V((512, 128), f32), V((512, 128), f32), D((6,)), D((6,))],
+        out_shape=(S((128, 1536), f32), S((1536, 512), bf), S((1536, 640), bf), S((512, 1536), bf)),
+        in_specs=[pl.BlockSpec(memory_space=pl.ANY)] * len(BACK_INPUTS),
+        out_specs=(pl.BlockSpec(memory_space=pltpu.VMEM),) * 4,
+        scratch_shapes=[V(shape, jnp.dtype(kind)) for shape, kind in BACK_INPUTS]
+        + [V((128, 1536), bf), V((4, 128, 1536), bf), V((6, 512, 512), f32), V((512, 384), bf), V((384, 512), f32),
+           V((512, 384), bf), V((512, 128), bf), V((512, 128), bf), V((512, 128), f32), V((512, 128), f32), D((6,)), D((6,)),
+           D((len(BACK_INPUTS),))],
         compiler_params=pltpu.CompilerParams(collective_id=cid, has_side_effects=True, vmem_limit_bytes=60 << 20),
         name="attention_back",
-    )(branch, rows, group, cosine, sine, bias, q, k, v, mixed, logsum, extras, wq, wk, wv, wo)
+    )(*operands)
 
 
 def grad_sum_kernel(o_sum, i_sum, n_part, o_out, i_out, n_out, nr1, nb, nr2, nsend, nrecv, *scratch):
@@ -701,7 +739,7 @@
         out_specs=(vm,) * 3,
         scratch_shapes=[V((2, 64, 1536), bf), V((2, 64, 1536), bf), V((2, 128, 1536), bf),
                         D((6,)), D((6,))] + sum_scratch(OUTPUT_PARTS) + sum_scratch(INPUT_PARTS),
-        compiler_params=pltpu.CompilerParams(collective_id=cid, has_side_effects=True, vmem_limit_bytes=40 << 20),
+        compiler_params=pltpu.CompilerParams(collective_id=cid, has_side_effects=True, vmem_limit_bytes=28 << 20),
         name="grad_sum",
     )(o_part.reshape(2, 4, 4, 48, 512), i_part.reshape(2, 4, 4, 48, 640), n_part.reshape(4, 128, 1536))
     return o_sums.reshape(1536, 512), i_sums.reshape(1536, 640), row_sums
@@ -946,7 +984,7 @@
         for cp in copies3(k) + copies4(k) + copies5(k) + copies6(k): cp.wait_send()
 
     def step(i, _):
-        for lag, st in ((8, stage7), (7, stage6), (5, stage5), (3, stage4), (1, stage2), (0, stage1)):
+        for lag, st in ((7, stage7), (6, stage6), (5, stage5), (3, stage4), (1, stage2), (0, stage1)):
             k = i - lag
             @pl.when((k >= 0) & (k < nk))
             def _():
@@ -964,7 +1002,7 @@
             def _():
                 ystage1(n // 2)
         return 0
-    lax.fori_loop(0, nk + 8, step, 0)
+    lax.fori_loop(0, nk + 7, step, 0)
 
 
 def expert_back(acts, x, u, gate, up, router, down, cid):
@@ -1050,53 +1088,19 @@
         *expert_weights,
         6,
     )
-    experts_index = jnp.arange(experts_all, dtype=jnp.int32)
-    second_normed, second_scale = normalize(residual, second_gain)
-    second_low = second_normed.astype(jnp.bfloat16)
-    def dense_gates(rows, routes):
-        named = jnp.any(routes[:, :, None] == experts_index[None, None, :], 1)
-        logits = jnp.dot(rows, router_weight, preferred_element_type=jnp.float32)
-        logits = jnp.where(named, logits, -1e30)
-        raised = jnp.exp(logits - jnp.max(logits, -1, keepdims=True))
-        return raised / jnp.sum(raised, -1, keepdims=True)
-
     sums, weight_grads, router_pairs = expert_back(
         acts, plane_rows, plane_upstream, *expert_weights, 2
     )
-    mixture, route_rows = sums[0], sums[1]
-    layer_output = (residual + mixture).astype(jnp.bfloat16)
-    router_pairs = router_pairs[:, :experts_all] + router_pairs[:, 64 : 64 + experts_all]
+    layer_output = (residual + sums[0]).astype(jnp.bfloat16)
     weight_grads = lax.all_gather(weight_grads, "dp", axis=0)
-    gates = dense_gates(second_low, expert_routes)
-    upstream = out_cotangent.astype(jnp.float32)
-    shared = gates * jnp.sum(mixture * upstream, -1, keepdims=True)
-    router_local = -jnp.einsum(
-        "td,te->de",
-        second_low.astype(jnp.float32),
-        shared,
-        precision=highest,
-        preferred_element_type=jnp.float32,
-    ) + router_pairs
-    normed_back = route_rows - jnp.einsum(
-        "te,de->td",
-        shared,
-        router_weight.astype(jnp.float32),
-        precision=highest,
-        preferred_element_type=jnp.float32,
-    )
-    residual_back, expert_gain_local = norm_back(residual, second_scale, second_gain, normed_back)
-    residual_grad = upstream + residual_back
-    small = jnp.concatenate(
-        [
-            router_local,
-            jnp.zeros((width, 1), jnp.float32),
-            expert_gain_local[:, None],
-            jnp.zeros((width, 126 - experts_all), jnp.float32),
-        ],
-        1,
-    )
-    output_part, input_part, normed_part = attention_back(
-        residual_grad.astype(jnp.bfloat16),
+    residual_grad, output_part, input_part, normed_part = attention_back(
+        sums,
+        residual,
+        out_cotangent,
+        expert_routes,
+        second_gain.reshape(1, width),
+        expert_weights[2],
+        router_pairs,
         group_rows,
         group_tokens.reshape(-1, width),
         *tables,
@@ -1105,13 +1109,11 @@
         values,
         attended,
         logsum,
-        small,
         *attention_weights,
-        7,
+        cid=7,
     )
     output_sums, input_sums, normed_grad = grad_sum(output_part, input_part, normed_part, 4)
-    input_back, _ = norm_back(inputs, first_scale, first_gain, normed_grad)
-    input_gradient = residual_grad + input_back
+    input_gradient = residual_grad + norm_back(inputs, first_scale, first_gain, normed_grad)
     (
         gate_gradient,
         up_gradient,

time: 374 us -> 365 us (0.976)
    unnamed x29 -> x26, local copies, waits for them, and re-layouts: 9.28 us -> 8.95 us
  transfers between devices with their start and end apart: 1 -> 1, of which waited for: 0 -> 0; matrix products, arithmetic and copies ran while one was open for 2% -> 1% of each run, Pallas kernels for 23% -> 24%
where the time goes in v1:
time: 365 us; the launch traced here: 358 us
  Pallas kernels  323 us (88%)
  between operations  14.6 us (4%)
  other arithmetic  10.5 us (3%)
  local copies, waits for them, and re-layouts  10.4 us (3%)
    pallas_call x1, Pallas kernels, front(): pl.pallas_call(front_kernel, out_shape=(S((n, width), f32), S((4, 4, 2, n...  123 us
    pallas_call x1, Pallas kernels, expert_back(): pl.pallas_call(expert_back_kernel, out_shape=(jax.ShapeDtypeStruct((2, 12...  108 us
    pallas_call x1, Pallas kernels, grad_sum(): pl.pallas_call(grad_sum_kernel, out_shape=(S((2, 4, 4, 48, 512), bf), S((...  58.2 us
    pallas_call x1, Pallas kernels, attention_back(): pl.pallas_call(attention_back_kernel, out_shape=(S((128, 1536), f32), S((...  26.7 us
    unnamed x26, local copies, waits for them, and re-layouts  8.95 us
  transfers between devices with their start and end apart: 1, of which 0 were waited for; matrix products, arithmetic and copies ran while one was open for 1% of the time, Pallas kernels for 24%

profile of v1, /device:TPU:1, one launch (start us, length us, event | category | flops | bytes accessed | tf_op | source)
XLA Modules:
  0.0 358.5 jit_solution(16741094034214735147)
XLA Ops:
  7.2 0.0 copy-start.11
  7.2 0.0 copy-start.9
  7.2 0.0 copy-start.10
  7.2 0.0 all-gather.3.cloned.1.call-start
  7.3 1.0 convert_reduce_fusion
  8.3 0.0 copy-start.7
  8.3 1.9 fusion.1.bias.refs_11_
  10.2 1.1 copy.34
  11.3 0.1 pad.10
  11.4 1.0 pad_maximum_fusion.router_hbm.refs_5_
  12.4 0.0 copy-done.11
  12.4 0.6 reshape.107.second_gain.refs_4_
  13.0 0.0 copy-done.9
  13.0 0.1 copy.32
  13.1 0.0 copy-done.10
  13.1 0.6 reshape.94.first_gain
  13.7 1.0 fusion.10
  14.7 0.0 copy-done.7
  14.7 0.8 fusion.9.u_own
  15.5 1.3 pad_maximum_fusion.1
  16.8 123.2 %front.1 = (f32[128,1536]{1,0:T(8,128)}, bf16[4,4,2,128,1536]{4,3,2,1,0:T(8,128)(2,1)}, bf16[4,4,2,128,2048]{4,3,2,1,0:T(8,128)(2,1)}, bf16[4,4,2,128,1664]{4,3,...) custom-call(bf16[128,1536]{1,0:T(8,128)(2,1)} %tokens.1, ...), custom_call_target="tpu_custom_call" | custom-call | tf_op jit(solution)/shard_map/front/pallas_call | solution.py:362
  140.0 108.1 %expert_back.1 = (f32[2,128,1536]{2,1,0:T(8,128)}, bf16[6,64,1920]{2,1,0:T(8,128)(2,1)}, f32[1536,128]{1,0:T(8,128)}) custom-call(bf16[4,4,2,128,2048]{4,3,2,1,0:T(8,128)(2,1)} %get-tuple-element.44.acts_hbm, bf16[4,4,2,128,1536]{4,3,2,1,0:T(8,128)(2,1)} %get-tuple-element.45.x_hbm, bf16[4,4,2,128,1664]{4,3,2,1,0:T(8,128)(2,1)} %get-tuple-element.46.u_hbm, ...), custom_call_target="tpu_custom_call" | custom-call | tf_op jit(solution)/shard_map/expert_back/pallas_call | solution.py:1015
  248.1 0.0 all-gather.3.cloned.1.call-update
  248.1 0.7 copy.35.refs_3_
  248.8 26.7 %attention_back.1 = (f32[128,1536]{1,0:T(8,128)}, bf16[1536,512]{1,0:T(8,128)(2,1)}, bf16[1536,640]{1,0:T(8,128)(2,1)}, bf16[512,1536]{1,0:T(8,128)(2,1)}) custom-call(f32[2,128,1536]{2,1,0:T(8,128)} %get-tuple-element.47.refs_0_, f32[128,1536]{1,0:T(8,128)} %get-tuple-element.43.refs_1_, bf16[128,1536]{1,0:T(8,128)(2,1)} %refs_2_.1, ...), custom_call_target="tpu_custom_call" | custom-call | tf_op jit(solution)/shard_map/attention_back/pallas_call | solution.py:650
  275.5 0.0 copy-start.1
  275.5 1.5 copy-done.1
  277.1 0.0 copy-start.2
  277.1 1.4 copy-done.2
  278.5 0.0 copy-start.3
  278.5 1.4 copy-done.3
  279.9 0.0 copy-start.4
  279.9 0.0 copy-start.5
  279.9 0.0 copy-start.6
  279.9 58.2 %grad_sum.1 = (bf16[2,4,4,48,512]{4,3,2,1,0:T(8,128)(2,1)S(1)}, bf16[2,4,4,48,640]{4,3,2,1,0:T(8,128)(2,1)S(1)}, f32[128,1536]{1,0:T(8,128)S(1)}) custom-call(bf16[2,4,4,48,512]{4,3,2,1,0:T(8,128)(2,1)S(1)} %bitcast.17, bf16[2,4,4,48,640]{4,3,2,1,0:T(8,128)(2,1)S(1)} %bitcast.15, bf16[4,128,1536]{2,1,0:T(8,128)(2,1)S(1)} %bitcast.18), custom_call_target="tpu_custom_call" | custom-call | tf_op jit(solution)/shard_map/grad_sum/pallas_call | solution.py:735
  338.2 0.0 copy-start.8
  338.2 0.0 copy-done.4
  338.2 0.2 fusion.3
  338.5 0.0 copy-done.5
  338.5 0.0 copy-done.6
  338.5 0.8 fusion.8
  339.3 0.0 copy-done.8
  339.3 1.2 fusion.6
  340.5 0.0 all-gather.3.cloned.1.call-done
  340.5 0.0 copy-start
  340.5 2.7 copy-done
  343.2 6.7 %finish.1 = (f32[5,1536,128]{2,1,0:T(8,128)}, f32[5,1536,128]{2,1,0:T(8,128)}, f32[5,128,1536]{2,1,0:T(8,128)}, f32[1536,384]{1,0:T(8,128)}, f32[1536,128]{1,0:T...) custom-call(bf16[4,6,64,1920]{3,2,1,0:T(8,128)(2,1)S(1)} %bitcast.13, ...), custom_call_target="tpu_custom_call" | custom-call | tf_op jit(solution)/shard_map/finish/pallas_call | solution.py:777
  350.0 0.6 reduce
  350.6 0.6 reduce.1
  (6 shorter events, 0.0 us)
Async XLA Ops:
  7.2 5.2 %copy-start.11 = (bf16[1536]{0:T(1024)(128)(2,1)S(1)}, bf16[1536]{0:T(1024)(128)(2,1)}, u32[]{:S(2)}) copy-start(bf16[1536]{0:T(1024)(128)(2,1)} %param.22) | copy-start | bytes 9220
  7.2 5.8 %copy-start.9 = (s32[128,8]{0,1:T(8,128)S(1)}, s32[128,8]{0,1:T(8,128)}, u32[]{:S(2)}) copy-start(s32[128,8]{0,1:T(8,128)} %param.16) | copy-start | bytes 12292
  7.2 5.9 %copy-start.10 = (bf16[1536]{0:T(1024)(128)(2,1)S(1)}, bf16[1536]{0:T(1024)(128)(2,1)}, u32[]{:S(2)}) copy-start(bf16[1536]{0:T(1024)(128)(2,1)} %param.17) | copy-start | bytes 9220
  7.2 333.3 %all-gather.3.cloned.1.call-start = ((), (), s32[]{:S(2)}) async-start(), calls=%async_computation | async-start | bytes 7372800 | tf_op jit(solution)/shard_map/all_gather | solution.py:1095
  8.3 6.4 %copy-start.7 = (bf16[128,1536]{1,0:T(8,128)(2,1)S(1)}, bf16[128,1536]{1,0:T(8,128)(2,1)}, u32[]{:S(2)}) copy-start(bf16[128,1536]{1,0:T(8,128)(2,1)} %refs_2_.1) | copy-start | bytes 1179652
  275.5 1.5 copy-start.1
  277.1 1.4 copy-start.2
  278.5 1.4 copy-start.3
  279.9 58.3 %copy-start.4 = (bf16[128,1536]{1,0:T(8,128)(2,1)S(1)}, bf16[128,1536]{1,0:T(8,128)(2,1)}, u32[]{:S(2)}) copy-start(bf16[128,1536]{1,0:T(8,128)(2,1)} %tokens.1) | copy-start | bytes 1179652
  279.9 58.5 %copy-start.5 = (f32[2,128,1536]{2,1,0:T(8,128)S(1)}, f32[2,128,1536]{2,1,0:T(8,128)}, u32[]{:S(2)}) copy-start(f32[2,128,1536]{2,1,0:T(8,128)} %get-tuple-element.47.refs_0_) | copy-start | bytes 4718596
  279.9 58.5 %copy-start.6 = (f32[128,1536]{1,0:T(8,128)S(1)}, f32[128,1536]{1,0:T(8,128)}, u32[]{:S(2)}) copy-start(f32[128,1536]{1,0:T(8,128)} %get-tuple-element.43.refs_1_) | copy-start | bytes 2359300
  338.2 1.1 copy-start.8
  340.5 2.7 copy-start
Sparse Core Ops, SparseCore 0:
  248.2 74.7 all-gather.2

commit v2 on v1

--- a/solution.py
+++ b/solution.py
@@ -890,6 +890,8 @@
         for cp in sibs(k): cp.start()
 
     def stage2(k):
+        @pl.when(k == 0)
+        def _(): act_load(c).wait()
         for cp in sibs(k): cp.wait()
         def put(r):
             q[k % 9] = (r.reshape(4, 4, 128, 256) + sib[k % 2].astype(f32)).astype(low)
@@ -897,8 +899,6 @@
         for cp in copies3(k): cp.start()
 
     def weight_part(k):
-        @pl.when(k == 0)
-        def _(): act_load(c).wait()
         @pl.when(k % 2 == 0)
         def _():
             for cp in x_load(0, k): cp.wait()
@@ -989,7 +989,7 @@
             @pl.when((k >= 0) & (k < nk))
             def _():
                 st(k)
-        n = i - 0
+        n = i - 1
         for lag, st in ((5, ystage3), (3, ystage2)):
             k = n - lag
             @pl.when((k >= 0) & (k < nk) & (k % 2 == 0))

time: 365 us -> 364 us (level)
  no operation moved by 1% of the time
where the time goes in v2:
time: 364 us; the launch traced here: 357 us
  Pallas kernels  321 us (88%)
  between operations  14.6 us (4%)
  other arithmetic  10.5 us (3%)
  local copies, waits for them, and re-layouts  10.4 us (3%)
    pallas_call x1, Pallas kernels, front(): pl.pallas_call(front_kernel, out_shape=(S((n, width), f32), S((4, 4, 2, n...  123 us
    pallas_call x1, Pallas kernels, expert_back(): pl.pallas_call(expert_back_kernel, out_shape=(jax.ShapeDtypeStruct((2, 12...  107 us
    pallas_call x1, Pallas kernels, grad_sum(): pl.pallas_call(grad_sum_kernel, out_shape=(S((2, 4, 4, 48, 512), bf), S((...  56.6 us
    pallas_call x1, Pallas kernels, attention_back(): pl.pallas_call(attention_back_kernel, out_shape=(S((128, 1536), f32), S((...  27.6 us
    unnamed x26, local copies, waits for them, and re-layouts  8.98 us
  transfers between devices with their start and end apart: 1, of which 0 were waited for; matrix products, arithmetic and copies ran while one was open for 1% of the time, Pallas kernels for 24%

profile of v2, /device:TPU:1, one launch (start us, length us, event | category | flops | bytes accessed | tf_op | source)
XLA Modules:
  0.0 357.0 jit_solution(4733477117569696358)
XLA Ops:
  7.2 0.0 copy-start.11
  7.2 0.0 copy-start.9
  7.2 0.0 copy-start.10
  7.2 0.0 all-gather.3.cloned.1.call-start
  7.3 1.0 convert_reduce_fusion
  8.3 0.0 copy-start.7
  8.3 1.9 fusion.1.bias.refs_11_
  10.2 1.1 copy.34
  11.3 0.1 pad.10
  11.4 1.0 pad_maximum_fusion.router_hbm.refs_5_
  12.4 0.0 copy-done.11
  12.4 0.6 reshape.107.second_gain.refs_4_
  13.0 0.0 copy-done.9
  13.0 0.1 copy.32
  13.1 0.0 copy-done.10
  13.1 0.6 reshape.94.first_gain
  13.7 1.0 fusion.10
  14.7 0.0 copy-done.7
  14.7 0.8 fusion.9.u_own
  15.5 1.3 pad_maximum_fusion.1
  16.8 123.2 %front.1 = (f32[128,1536]{1,0:T(8,128)}, bf16[4,4,2,128,1536]{4,3,2,1,0:T(8,128)(2,1)}, bf16[4,4,2,128,2048]{4,3,2,1,0:T(8,128)(2,1)}, bf16[4,4,2,128,1664]{4,3,...) custom-call(bf16[128,1536]{1,0:T(8,128)(2,1)} %tokens.1, ...), custom_call_target="tpu_custom_call" | custom-call | tf_op jit(solution)/shard_map/front/pallas_call | solution.py:362
  140.0 107.3 %expert_back.1 = (f32[2,128,1536]{2,1,0:T(8,128)}, bf16[6,64,1920]{2,1,0:T(8,128)(2,1)}, f32[1536,128]{1,0:T(8,128)}) custom-call(bf16[4,4,2,128,2048]{4,3,2,1,0:T(8,128)(2,1)} %get-tuple-element.44.acts_hbm, bf16[4,4,2,128,1536]{4,3,2,1,0:T(8,128)(2,1)} %get-tuple-element.45.x_hbm, bf16[4,4,2,128,1664]{4,3,2,1,0:T(8,128)(2,1)} %get-tuple-element.46.u_hbm, ...), custom_call_target="tpu_custom_call" | custom-call | tf_op jit(solution)/shard_map/expert_back/pallas_call | solution.py:1015
  247.3 0.0 all-gather.3.cloned.1.call-update
  247.3 0.7 copy.35.refs_3_
  248.0 27.6 %attention_back.1 = (f32[128,1536]{1,0:T(8,128)}, bf16[1536,512]{1,0:T(8,128)(2,1)}, bf16[1536,640]{1,0:T(8,128)(2,1)}, bf16[512,1536]{1,0:T(8,128)(2,1)}) custom-call(f32[2,128,1536]{2,1,0:T(8,128)} %get-tuple-element.47.refs_0_, f32[128,1536]{1,0:T(8,128)} %get-tuple-element.43.refs_1_, bf16[128,1536]{1,0:T(8,128)(2,1)} %refs_2_.1, ...), custom_call_target="tpu_custom_call" | custom-call | tf_op jit(solution)/shard_map/attention_back/pallas_call | solution.py:650
  275.7 0.0 copy-start.1
  275.7 1.6 copy-done.1
  277.3 0.0 copy-start.2
  277.3 1.4 copy-done.2
  278.7 0.0 copy-start.3
  278.7 1.4 copy-done.3
  280.1 0.0 copy-start.4
  280.1 0.0 copy-start.5
  280.1 0.0 copy-start.6
  280.1 56.6 %grad_sum.1 = (bf16[2,4,4,48,512]{4,3,2,1,0:T(8,128)(2,1)S(1)}, bf16[2,4,4,48,640]{4,3,2,1,0:T(8,128)(2,1)S(1)}, f32[128,1536]{1,0:T(8,128)S(1)}) custom-call(bf16[2,4,4,48,512]{4,3,2,1,0:T(8,128)(2,1)S(1)} %bitcast.17, bf16[2,4,4,48,640]{4,3,2,1,0:T(8,128)(2,1)S(1)} %bitcast.15, bf16[4,128,1536]{2,1,0:T(8,128)(2,1)S(1)} %bitcast.18), custom_call_target="tpu_custom_call" | custom-call | tf_op jit(solution)/shard_map/grad_sum/pallas_call | solution.py:735
  336.7 0.0 copy-start.8
  336.7 0.0 copy-done.4
  336.7 0.2 fusion.3
  337.0 0.0 copy-done.5
  337.0 0.0 copy-done.6
  337.0 0.8 fusion.8
  337.8 0.0 copy-done.8
  337.8 1.2 fusion.6
  339.0 0.0 all-gather.3.cloned.1.call-done
  339.0 0.0 copy-start
  339.0 2.7 copy-done
  341.7 6.7 %finish.1 = (f32[5,1536,128]{2,1,0:T(8,128)}, f32[5,1536,128]{2,1,0:T(8,128)}, f32[5,128,1536]{2,1,0:T(8,128)}, f32[1536,384]{1,0:T(8,128)}, f32[1536,128]{1,0:T...) custom-call(bf16[4,6,64,1920]{3,2,1,0:T(8,128)(2,1)S(1)} %bitcast.13, ...), custom_call_target="tpu_custom_call" | custom-call | tf_op jit(solution)/shard_map/finish/pallas_call | solution.py:777
  348.5 0.6 reduce
  349.1 0.6 reduce.1
  (6 shorter events, 0.0 us)
Async XLA Ops:
  7.2 5.2 %copy-start.11 = (bf16[1536]{0:T(1024)(128)(2,1)S(1)}, bf16[1536]{0:T(1024)(128)(2,1)}, u32[]{:S(2)}) copy-start(bf16[1536]{0:T(1024)(128)(2,1)} %param.22) | copy-start | bytes 9220
  7.2 5.8 %copy-start.9 = (s32[128,8]{0,1:T(8,128)S(1)}, s32[128,8]{0,1:T(8,128)}, u32[]{:S(2)}) copy-start(s32[128,8]{0,1:T(8,128)} %param.16) | copy-start | bytes 12292
  7.2 5.9 %copy-start.10 = (bf16[1536]{0:T(1024)(128)(2,1)S(1)}, bf16[1536]{0:T(1024)(128)(2,1)}, u32[]{:S(2)}) copy-start(bf16[1536]{0:T(1024)(128)(2,1)} %param.17) | copy-start | bytes 9220
  7.2 331.8 %all-gather.3.cloned.1.call-start = ((), (), s32[]{:S(2)}) async-start(), calls=%async_computation | async-start | bytes 7372800 | tf_op jit(solution)/shard_map/all_gather | solution.py:1095
  8.3 6.4 %copy-start.7 = (bf16[128,1536]{1,0:T(8,128)(2,1)S(1)}, bf16[128,1536]{1,0:T(8,128)(2,1)}, u32[]{:S(2)}) copy-start(bf16[128,1536]{1,0:T(8,128)(2,1)} %refs_2_.1) | copy-start | bytes 1179652
  275.7 1.6 copy-start.1
  277.3 1.4 copy-start.2
  278.7 1.4 copy-start.3
  280.1 56.6 %copy-start.4 = (bf16[128,1536]{1,0:T(8,128)(2,1)S(1)}, bf16[128,1536]{1,0:T(8,128)(2,1)}, u32[]{:S(2)}) copy-start(bf16[128,1536]{1,0:T(8,128)(2,1)} %tokens.1) | copy-start | bytes 1179652
  280.1 56.9 %copy-start.5 = (f32[2,128,1536]{2,1,0:T(8,128)S(1)}, f32[2,128,1536]{2,1,0:T(8,128)}, u32[]{:S(2)}) copy-start(f32[2,128,1536]{2,1,0:T(8,128)} %get-tuple-element.47.refs_0_) | copy-start | bytes 4718596
  280.1 56.9 %copy-start.6 = (f32[128,1536]{1,0:T(8,128)S(1)}, f32[128,1536]{1,0:T(8,128)}, u32[]{:S(2)}) copy-start(f32[128,1536]{1,0:T(8,128)} %get-tuple-element.43.refs_1_) | copy-start | bytes 2359300
  336.7 1.1 copy-start.8
  339.0 2.7 copy-start
Sparse Core Ops, SparseCore 0:
  247.4 72.9 all-gather.2
